TPU v7x, 128 devices: a whole 4x4x4 slice. The times are simulated.
128 devices in a mesh: dp: 8 (over z_lo, x), tile: 16 (over z_hi, y, core).
Axes of the slice: x: 4, y: 4, z: 4 (z_hi: 2, z_lo: 2; z = z_hi * 2 + z_lo), core: 2. Of those that a mesh axis runs over, the one named last changes fastest.
Arguments:
- fields: bfloat16 [8, 16, 64, 64, 192], P('dp', 'tile'), may hold values from -6 to 6
- cotangent: bfloat16 [8, 16, 64, 64, 192], P('dp', 'tile'), may hold values from -6 to 6
- kernel: float32 [7, 7, 192], replicated, may hold values from -0.875 to 0.875
- conv_bias: float32 [192], replicated, may hold values from -3 to 3
- norm_gain: float32 [192], replicated, may hold values from 0.5 to 1.5
- norm_bias: float32 [192], replicated, may hold values from -3 to 3
- w_expand: bfloat16 [192, 384], replicated, may hold values from -0.4375 to 0.4375
- bias_expand: float32 [384], replicated, may hold values from -3 to 3
- w_reduce: bfloat16 [384, 192], replicated, may hold values from -0.3125 to 0.3125
- bias_reduce: float32 [192], replicated, may hold values from -3 to 3
- layer_scale: float32 [192], replicated, may hold values from 0.5 to 1.5
- neighbors: int32 [16, 8], replicated, may hold values from -1 to 15, as said below
- rotations: int32 [16, 8], replicated, may hold values from 0 to 3, as said below
Outputs:
- mixed: bfloat16 [8, 16, 64, 64, 192], P('dp', 'tile')
- input_grad: bfloat16 [8, 16, 64, 64, 192], P('dp', 'tile')
- kernel_grad: float32 [7, 7, 192], replicated
- expand_grad: float32 [192, 384], replicated
- reduce_grad: float32 [384, 192], replicated
Inputs may be any that keep to these rules, and one draw needn't show every extreme that they name: `neighbors`: Sub-tile numbers of the neighbours in the sub-tile's own frame, from the adjacency of a closed strip of faces of 2 x 2 sub-tiles in a numbering drawn from the seed; -1 marks a missing corner neighbour where faces meet at a vertex, edges are never missing. `rotations`: zero between sub-tiles of one face.
All inputs are finite; a program needn't handle non-finite values.
Results may differ from a plain program's by a relative error of at most 0.0065.
Values may be sent and summed in bfloat16 or wider, within the bound.
A program may use at most 128 MiB of HBM per device.

v0:
```python
import math

import jax
import jax.numpy as jnp
from jax import lax
from jax.sharding import PartitionSpec as P

OFFSETS = (2, 3, 0, 1, 2, 0, 0, 2)


def for_sending(x):

    def short(part):
        return part.astype(jnp.bfloat16) if part.dtype == jnp.float32 else part

    return jax.tree.map(short, x)


def tile_bands(field, width):
    side = field.shape[0]
    return jnp.stack(
        [
            field[:width],
            jnp.rot90(field[:, side - width :], 1, (0, 1)),
            jnp.rot90(field[side - width :], 2, (0, 1)),
            jnp.rot90(field[:, :width], 3, (0, 1)),
        ]
    )


def pad_tile(field, picked):
    width = picked.shape[1]
    side = field.shape[0]
    north = jnp.rot90(picked[0], 2, (0, 1))
    east = jnp.rot90(picked[1], 1, (0, 1))
    south = picked[2]
    west = jnp.rot90(picked[3], 3, (0, 1))
    north_east = jnp.rot90(picked[4], 2, (0, 1))[:, :width]
    south_east = picked[5][:, :width]
    south_west = picked[6][:, side - width :]
    north_west = jnp.rot90(picked[7], 2, (0, 1))[:, side - width :]
    upper = jnp.concatenate([north_west, north, north_east], axis=1)
    middle = jnp.concatenate([west, field, east], axis=1)
    lower = jnp.concatenate([south_west, south, south_east], axis=1)
    return jnp.concatenate([upper, middle, lower], axis=0)


def bands_back(band_grad):
    width = band_grad.shape[1]
    side = band_grad.shape[2]
    zero_field = jnp.zeros((side, side, band_grad.shape[3]), jnp.float32)
    return jax.vjp(lambda f: tile_bands(f, width), zero_field)[1](band_grad)[0]


def pad_back(padded_grad, width):
    side = padded_grad.shape[0] - 2 * width
    channels = padded_grad.shape[2]
    zero_field = jnp.zeros((side, side, channels), jnp.float32)
    zero_picked = jnp.zeros((8, width, side, channels), jnp.float32)
    return jax.vjp(pad_tile, zero_field, zero_picked)[1](padded_grad)


def block_batch(
    padded,
    fields,
    cotangent,
    kernel,
    conv_bias,
    norm_gain,
    norm_bias,
    w_expand,
    bias_expand,
    w_reduce,
    bias_reduce,
    layer_scale,
):
    count = fields.shape[0]
    side = fields.shape[1]
    channels = fields.shape[3]
    ksize = kernel.shape[0]
    conv_out = conv_bias
    for row_off in range(ksize):
        for col_off in range(ksize):
            conv_out = (
                conv_out
                + padded[:, row_off : row_off + side, col_off : col_off + side].astype(jnp.float32)
                * kernel[row_off, col_off]
            )
    row_mean = jnp.mean(conv_out, axis=-1, keepdims=True)
    shifted = conv_out - row_mean
    inv_std = lax.rsqrt(jnp.mean(shifted * shifted, axis=-1, keepdims=True) + 1e-06)
    centred = shifted * inv_std
    normed = (centred * norm_gain + norm_bias).astype(jnp.bfloat16)
    normed_rows = normed.reshape(-1, channels)
    pre_act = jnp.dot(normed_rows, w_expand, preferred_element_type=jnp.float32) + bias_expand
    phi_value = 0.5 * (1.0 + jax.scipy.special.erf(pre_act * 0.7071067811865476))
    activated = (pre_act * phi_value).astype(jnp.bfloat16)
    branch = jnp.dot(activated, w_reduce, preferred_element_type=jnp.float32) + bias_reduce
    mixed = (fields.astype(jnp.float32) + layer_scale * branch.reshape(fields.shape)).astype(
        jnp.bfloat16
    )
    branch_grad = (
        (layer_scale * cotangent.astype(jnp.float32)).reshape(-1, channels).astype(jnp.bfloat16)
    )
    reduce_grad = jnp.dot(activated.T, branch_grad, preferred_element_type=jnp.float32)
    act_grad = jnp.dot(branch_grad, w_reduce.T, preferred_element_type=jnp.float32)
    density = jnp.exp(-0.5 * pre_act * pre_act) * 0.3989422804014327
    pre_grad = (act_grad * (phi_value + pre_act * density)).astype(jnp.bfloat16)
    expand_grad = jnp.dot(normed_rows.T, pre_grad, preferred_element_type=jnp.float32)
    normed_grad = (
        jnp.dot(pre_grad, w_expand.T, preferred_element_type=jnp.float32).reshape(conv_out.shape)
        * norm_gain
    )
    conv_grad = inv_std * (
        normed_grad
        - jnp.mean(normed_grad, axis=-1, keepdims=True)
        - centred * jnp.mean(normed_grad * centred, axis=-1, keepdims=True)
    )
    grown = jnp.pad(conv_grad, ((0, 0), (ksize - 1, ksize - 1), (ksize - 1, ksize - 1), (0, 0)))
    extent = side + ksize - 1
    padded_grad = jnp.zeros((count, extent, extent, channels), jnp.float32)
    kernel_terms = []
    for row_off in range(ksize):
        for col_off in range(ksize):
            low_row = ksize - 1 - row_off
            low_col = ksize - 1 - col_off
            padded_grad = (
                padded_grad
                + kernel[row_off, col_off]
                * grown[:, low_row : low_row + extent, low_col : low_col + extent]
            )
            window = padded[:, row_off : row_off + side, col_off : col_off + side].astype(
                jnp.float32
            )
            kernel_terms.append(jnp.sum(window * conv_grad, axis=(0, 1, 2)))
    kernel_grad = jnp.stack(kernel_terms).reshape(ksize, ksize, channels)
    return (mixed, padded_grad, (kernel_grad, expand_grad, reduce_grad))


def on_device(
    fields,
    cotangent,
    kernel,
    conv_bias,
    norm_gain,
    norm_bias,
    w_expand,
    bias_expand,
    w_reduce,
    bias_reduce,
    layer_scale,
    neighbors,
    rotations,
):
    samples, local_tiles, side, _, channels = fields.shape
    width = kernel.shape[0] // 2
    all_tiles = neighbors.shape[0]
    first_tile = lax.axis_index("tile") * local_tiles
    offsets = jnp.array(OFFSETS, jnp.int32)[None, :]
    targets_all = jnp.where(neighbors >= 0, neighbors * 4 + (rotations + offsets) % 4, -1)
    own_targets = lax.dynamic_slice_in_dim(targets_all, first_tile, local_tiles, 0)
    own_valid = (own_targets >= 0)[None, :, :, None, None, None]
    band_set = jax.vmap(jax.vmap(lambda f: tile_bands(f, width)))(fields)
    everyone = jax.tree.map(
        lambda part, own: part.astype(own.dtype),
        lax.all_gather(for_sending(band_set), "tile", axis=1, tiled=True),
        band_set,
    )
    flat_bands = everyone.reshape(samples, all_tiles * 4, width, side, channels)
    picked = jnp.take(flat_bands, jnp.maximum(own_targets, 0).reshape(-1), axis=1)
    picked = picked.reshape(samples, local_tiles, 8, width, side, channels)
    picked = jnp.where(own_valid, picked, jnp.zeros((), jnp.bfloat16))
    padded = jax.vmap(jax.vmap(pad_tile))(fields, picked)
    flat_count = samples * local_tiles
    extent = side + 2 * width
    mixed, padded_grad, grads = block_batch(
        padded.reshape(flat_count, extent, extent, channels),
        fields.reshape(flat_count, side, side, channels),
        cotangent.reshape(flat_count, side, side, channels),
        kernel,
        conv_bias,
        norm_gain,
        norm_bias,
        w_expand,
        bias_expand,
        w_reduce,
        bias_reduce,
        layer_scale,
    )
    field_grad, picked_grad = jax.vmap(lambda g: pad_back(g, width))(padded_grad)
    picked_grad = picked_grad.reshape(samples, local_tiles, 8, width, side, channels)
    picked_grad = jnp.where(own_valid, picked_grad, jnp.zeros((), jnp.float32))
    operand = jnp.zeros((samples, all_tiles * 4, width, side, channels), jnp.float32)
    operand = operand.at[:, jnp.maximum(own_targets, 0).reshape(-1)].add(
        picked_grad.reshape(samples, local_tiles * 8, width, side, channels)
    )
    returned = lax.psum_scatter(
        operand.reshape(samples, all_tiles, 4, width, side, channels).astype(jnp.bfloat16),
        "tile",
        scatter_dimension=1,
        tiled=True,
    ).astype(jnp.float32)
    back = jax.vmap(jax.vmap(bands_back))(returned)
    input_grad = (cotangent.astype(jnp.float32) + field_grad.reshape(fields.shape) + back).astype(
        jnp.bfloat16
    )
    totals = lax.psum((grads[0], grads[1], grads[2]), ("dp", "tile"))
    scale = 1.0 / math.sqrt(samples * lax.axis_size("dp") * all_tiles * side * side)
    return (
        mixed.reshape(fields.shape),
        input_grad,
        totals[0] * scale,
        totals[1] * scale,
        totals[2] * scale,
    )


def solution(mesh):
    return jax.shard_map(
        on_device,
        mesh=mesh,
        in_specs=(
            P("dp", "tile", None, None, None),
            P("dp", "tile", None, None, None),
            P(),
            P(),
            P(),
            P(),
            P(),
            P(),
            P(),
            P(),
            P(),
            P(),
            P(),
        ),
        out_specs=(
            P("dp", "tile", None, None, None),
            P("dp", "tile", None, None, None),
            P(),
            P(),
            P(),
        ),
        check_vma=False,
    )
```

profile of v0, /device:TPU:1, one launch (start us, length us, event | category | flops | bytes accessed | tf_op | source)
XLA Modules:
  0.0 527.6 jit_solution(9652333701291859985)
XLA Ops:
  17.3 61.8 %all-gather.3.cloned.1.call-done = bf16[64,1,1,3,64,192]{5,4,3,2,1,0:T(8,128)(2,1)} async-done(((bf16[4,1,1,3,64,192]{5,4,3,2,1,0:T(8,128)(2,1)}), bf16[64,1,1,3,64,192]{5,4,3,2,1,0:T(8,128)(2,1)}) %all-gather.3.cloned.1.call-update) | async-done | bytes 4718608 | tf_op jit(solution)/shard_map/all_gather | solution.py:166
  79.0 3.4 gather_fusion
  86.1 32.4 %fusion.210 = (f32[64,64]{1,0:T(8,128)S(1)}, f32[1,64,64,192]{3,2,1,0:T(8,128)S(1)}) fusion(f32[192]{0:T(256)S(1)} %bitcast.235, bf16[1,70,70,192]{3,2,1,0:T(8,128)(2,1)S(1)} %maximum_bitcast_fusion, f32[192]{0:T(256)S(1)} %bitcast.237, f32[192]{0:T(256)S(1)} %bitcast.241, f32[192]{0:T(256)S(1)} %bitcast.243, f32[192]{0:T(256)S(1)} %bitcast.245, ...), kind=kLoop, calls=%fused_computation.415 | loop fusion | flops 116387840 | bytes 80270848 | tf_op jit(solution)/shard_map/reduce_sum | solution.py:89
  121.4 3.3 multiply_convert_fusion
  124.8 3.2 fusion.5
  129.8 3.0 multiply_reduce_fusion.2
  132.9 5.1 copy.44
  138.0 4.7 multiply_reduce_fusion
  143.9 13.9 %fusion.200 = (f32[192]{0:T(256)S(1)}, f32[192]{0:T(256)S(1)}, f32[192]{0:T(256)S(1)}, f32[192]{0:T(256)S(1)}, f32[192]{0:T(256)S(1)}, /*index=5*/f32[192]{0:T(2...) fusion(bf16[1,70,70,192]{3,2,1,0:T(8,128)(2,1)S(1)} %maximum_bi, ...), kind=kLoop, calls=%fused_computation.354 | loop fusion | flops 47968896 | bytes 37828864 | tf_op jit(solution)/shard_map/reduce_sum | solution.py:135
  157.8 109.9 %fusion.101 = f32[1,70,70,192]{3,2,1,0:T(8,128)} fusion(f32[1,64,64,192]{3,2,1,0:T(8,128)} %get-tuple-element.56, f32[192]{0:T(256)S(1)} %bitcast.236, f32[192]{0:T(256)S(1)} %bitcast.238, f32[192]{0:T(256)S(1)} %bitcast.242, f32[192]{0:T(256)S(1)} %bitcast.244, f32[192]{0:T(256)S(1)} %bitcast.246, f32[192]{0:T(256)S(1)} %bitcast.248, f32[192]{0:T(256)S(1)} %bitcast.250, ...), kind=kLoop, calls=%fused_computation.255 | loop fusion | flops 91257600 | bytes 6946560 | tf_op jit(solution)/shard_map/add | solution.py:128
  271.6 4.3 fusion.219
  280.3 2.8 select_bitcast_fusion
  283.0 6.2 %broadcast.303 = f32[64,3,64,192]{3,2,1,0:T(8,128)} broadcast(f32[]{:T(128)} %constant.34.clone.1), dimensions={} | broadcast | bytes 9437188 | tf_op jit(solution)/shard_map/broadcast_in_dim | solution.py:193
  289.2 4.5 scatter_fusion
  293.7 8.2 %convert_element_type.317 = bf16[64,3,64,192]{3,2,1,0:T(8,128)(2,1)} convert(f32[64,3,64,192]{3,2,1,0:T(8,128)} %scatter_fusion) | non-fusion elementwise | flops 2359296 | bytes 14155776 | tf_op jit(solution)/shard_map/convert_element_type | solution.py:198
  302.8 4.8 convolution_add_fusion.1
  307.6 5.1 copy.43
  312.7 10.2 %fusion.140 = (f32[192]{0:T(256)S(1)}, f32[192]{0:T(256)S(1)}, f32[192]{0:T(256)S(1)}, f32[192]{0:T(256)S(1)}, f32[192]{0:T(256)S(1)}, /*index=5*/f32[192]{0:T(2...) fusion(f32[1,64,64,192]{3,2,1,0:T(8,128)} %get-tuple-element.56, ...), kind=kLoop, calls=%fused_computation.294 | loop fusion | flops 30668352 | bytes 23602944 | tf_op jit(solution)/shard_map/reduce_sum | solution.py:135
  323.0 12.7 %fusion.182 = (f32[192]{0:T(256)S(1)}, f32[192]{0:T(256)S(1)}, f32[192]{0:T(256)S(1)}, f32[192]{0:T(256)S(1)}, f32[192]{0:T(256)S(1)}, /*index=5*/f32[192]{0:T(2...) fusion(f32[1,64,64,192]{3,2,1,0:T(8,128)S(1)} %copy-done.4, ...), kind=kLoop, calls=%fused_computation.336 | loop fusion | flops 42463872 | bytes 31471104 | tf_op jit(solution)/shard_map/reduce_sum | solution.py:135
  335.9 64.9 %psum.21 = f32[7,7,192]{2,1,0:T(8,128)S(1)} all-reduce(f32[7,7,192]{2,1,0:T(8,128)S(1)} %reshape.473), channel_id=1, replica_groups=mesh['dp'=8,'tile'=16] {'dp','tile'}, use_global_device_ids=true, to_apply=%region_55.56 | all-reduce | flops 9408 | bytes 75264 | tf_op jit(solution)/shard_map/psum | solution.py:207
  401.4 5.0 add_convert_fusion
  406.4 13.2 %all-reduce.20.cloned.1.call-done = (f32[192,384]{1,0:T(8,128)}, f32[384,192]{0,1:T(8,128)}) async-done(((f32[192,384]{1,0:T(8,128)}, f32[384,192]{0,1:T(8,128)}), (f32[192,384]{1,0:T(8,128)}, f32[384,192]{0,1:T(8,128)})) %all-reduce.20.cloned.1.call-update) | async-done | bytes 589840 | tf_op jit(solution)/shard_map/psum | solution.py:207
  423.0 88.1 %reduce-scatter.2.cloned.1.call-done = bf16[1,1,4,3,64,192]{5,4,3,2,1,0:T(8,128)(2,1)} async-done(((bf16[1,16,4,3,64,192]{5,4,3,2,1,0:T(8,128)(2,1)}), bf16[1,1,4,3,64,192]{5,4,3,2,1,0:T(8,128)(2,1)}) %reduce-scatter.2.cloned.1.call-update) | async-done | bytes 294928 | tf_op jit(solution)/shard_map/reduce_scatter | solution.py:197
  514.6 6.5 %fusion.203 = bf16[1,1,64,64,192]{4,3,2,1,0:T(8,128)(2,1)} fusion(f32[1,70,70,192]{3,2,1,0:T(8,128)} %fusion.101, f32[1,1,64,64,192]{4,2,3,1,0:T(8,128)S(1)} %pad_add_fusion, f32[1,1,3,64,192]{4,3,2,1,0:T(8,128)S(1)} %get-tuple-element.71, bf16[1,1,64,64,192]{4,3,2,1,0:T(8,128)(2,1)S(1)} %copy-done.7), kind=kLoop, calls=%fused_computation.358 | loop fusion | flops 3932160 | bytes 9584640 | tf_op jit(solution)/shard_map/convert_element_type | solution.py:204
  (106 shorter events, 36.2 us)
Async XLA Ops:
  7.2 114.2 %copy-start = (bf16[192,384]{1,0:T(8,128)(2,1)S(1)}, bf16[192,384]{1,0:T(8,128)(2,1)}, u32[]{:S(2)}) copy-start(bf16[192,384]{1,0:T(8,128)(2,1)} %param.20) | copy-start | bytes 442372
  7.2 7.7 %copy-start.6 = (bf16[1,1,64,64,192]{4,3,2,1,0:T(8,128)(2,1)S(1)}, bf16[1,1,64,64,192]{4,3,2,1,0:T(8,128)(2,1)}, u32[]{:S(2)}) copy-start(bf16[1,1,64,64,192]{4,3,2,1,0:T(8,128)(2,1)} %param.15) | copy-start | bytes 4718596
  7.2 71.8 %all-gather.3.cloned.1.call-start = ((), (), s32[]{:S(2)}) async-start(), calls=%async_computation.2 | async-start | bytes 6684672 | tf_op jit(solution)/shard_map/all_gather | solution.py:166
  10.7 408.9 %all-reduce.20.cloned.1.call-start = ((), (), s32[]{:S(2)}) async-start(), calls=%async_computation.3 | async-start | bytes 1179648 | tf_op jit(solution)/shard_map/psum | solution.py:207
  82.6 3.5 copy-start.15
  118.5 2.9 copy-start.2
  118.5 1.4 copy-start.11
  118.5 1.4 copy-start.16
  119.8 1.6 copy-start.12
  121.4 3.4 copy-start.8
  121.4 3.3 copy-start.9
  138.0 4.7 copy-start.3
  138.0 5.9 %copy-start.5 = (f32[4096,192]{1,0:T(8,128)S(1)}, f32[4096,192]{1,0:T(8,128)}, u32[]{:S(2)}) copy-start(f32[4096,192]{1,0:T(8,128)} %copy.44) | copy-start | bytes 9437188
  276.0 235.2 %reduce-scatter.2.cloned.1.call-start = ((), (), s32[]{:S(2)}) async-start(), calls=%async_computation.1 | async-start | bytes 6684672 | tf_op jit(solution)/shard_map/reduce_scatter | solution.py:197
  301.9 0.9 copy-start.10
  301.9 0.9 copy-start.13
  312.7 10.2 %copy-start.4 = (f32[1,64,64,192]{3,2,1,0:T(8,128)S(1)}, f32[1,64,64,192]{3,2,1,0:T(8,128)}, u32[]{:S(2)}) copy-start(f32[1,64,64,192]{3,2,1,0:T(8,128)} %get-tuple-element.56) | copy-start | bytes 9437188
  323.0 78.5 %copy-start.14 = (f32[192]{0:T(256)S(1)}, f32[192]{0:T(256)}, u32[]{:S(2)}) copy-start(f32[192]{0:T(256)} %param.24) | copy-start | bytes 2308
  512.2 2.4 copy-start.7
  514.6 6.5 %copy-start.1 = (bf16[192,384]{1,0:T(8,128)(2,1)S(1)}, bf16[192,384]{1,0:T(8,128)(2,1)}, u32[]{:S(2)}) copy-start(bf16[192,384]{1,0:T(8,128)(2,1)} %param.20) | copy-start | bytes 442372
Sparse Core Ops, SparseCore 0:
  11.1 67.9 all-gather.2
  276.1 143.4 all-reduce.19
  424.3 86.7 reduce-scatter.1
where the time goes:
time: 529 us; the launch traced here: 528 us
  other arithmetic  227 us (43%)
  waiting for transfers between devices  163 us (31%)
  blocking collectives  64.9 us (12%)
  local copies, waits for them, and re-layouts  38.2 us (7%)
  matrix products  20.4 us (4%)
  between operations  14.3 us (3%)
    add x1, other arithmetic, block_batch(): padded_grad + kernel[row_off, col_off] * grown[:, low_row:low_row + exten...  110 us
    reduce_scatter x1, waiting for transfers between devices, on_device(): lax.psum_scatter(operand.reshape(samples, all_tiles, 4, width, side, chan...  88.1 us
    psum x1, blocking collectives, on_device(): totals = lax.psum((grads[0], grads[1], grads[2]), ('dp', 'tile'))  64.9 us
    all_gather x1, waiting for transfers between devices, on_device(): lax.all_gather(for_sending(band_set), 'tile', axis=1, tiled=True)  61.8 us
    reduce_sum x3, other arithmetic, block_batch(): kernel_terms.append(jnp.sum(window * conv_grad, axis=(0, 1, 2)))  36.8 us
    reduce_sum x1, other arithmetic, block_batch(): row_mean = jnp.mean(conv_out, axis=-1, keepdims=True)  32.4 us
    psum x1, waiting for transfers between devices, on_device(): totals = lax.psum((grads[0], grads[1], grads[2]), ('dp', 'tile'))  13.2 us
  transfers between devices with their start and end apart: 3, of which 3 were waited for; matrix products, arithmetic and copies ran while one was open for 14% of the time, Pallas kernels for 0%

commit v1 on v0

v1 whole, which is shorter than its diff:
```python
import functools
import math

import jax
import jax.numpy as jnp
import numpy as np
from jax import lax
from jax.experimental import pallas as pl
from jax.experimental.pallas import tpu as pltpu
from jax.sharding import PartitionSpec as P

OFFSETS = (2, 3, 0, 1, 2, 0, 0, 2)
SIDE = 64
W = 3
CH = 192
HID = 384
TILES = 16
CELLS = 16
NFREQ = 40
KROW = 80
EXT = SIDE + 2 * W
BF = jnp.bfloat16
F32 = jnp.float32
MESH = pl.DeviceIdType.MESH
WROWS = 1280
WBLOCK = WROWS // TILES


def stripe_table():
    where = np.zeros((W, SIDE, 2), np.int64)
    used = {i: set() for i in range(16)}
    rest = []
    for w in range(W):
        for l in range(SIDE):
            if l < W:
                spot = (w * W + l, 0)
            elif l >= SIDE - W:
                spot = (7 + w * W + l - (SIDE - W), 11)
            else:
                rest.append((w, l))
                continue
            where[w, l] = spot
            used[spot[0]].add(spot[1])
    free = [(i, a) for i in range(16) for a in range(12) if a not in used[i]]
    for (w, l), spot in zip(rest, free):
        where[w, l] = spot
    return where


def np_pad(field, picked):
    north = np.rot90(picked[0], 2)
    east = np.rot90(picked[1], 1)
    south = picked[2]
    west = np.rot90(picked[3], 3)
    ne = np.rot90(picked[4], 2)[:, :W]
    se = picked[5][:, :W]
    sw = picked[6][:, SIDE - W :]
    nw = np.rot90(picked[7], 2)[:, SIDE - W :]
    return np.concatenate(
        [
            np.concatenate([nw, north, ne], 1),
            np.concatenate([west, field, east], 1),
            np.concatenate([sw, south, se], 1),
        ],
        0,
    )


def column_of(m):
    if m < SIDE:
        return m + W
    if m < SIDE + W:
        return m - SIDE
    if m < SIDE + 2 * W:
        return m
    return -1


@functools.lru_cache(None)
def static_tables():
    where = stripe_table()
    codes = np.arange(8 * W * SIDE).reshape(8, W, SIDE)
    padded = np_pad(np.full((SIDE, SIDE), -1), codes)

    def spot(code):
        k, w, l = np.unravel_index(code, (8, W, SIDE))
        i, a = where[w, l]
        return (k, i * CELLS + a) if k < 4 else (k - 4, i * CELLS + 12)

    def rows(p_list, m_list, slots):
        mats = {k: np.zeros((len(p_list) * len(m_list), 256), np.float32) for k in slots}
        for ip, p in enumerate(p_list):
            for im, m in enumerate(m_list):
                q = column_of(m)
                if q < 0 or padded[p, q] < 0:
                    continue
                k, row = spot(padded[p, q])
                mats[k][ip * len(m_list) + im, row] = 1
        return [mats[k] for k in slots]

    top0, top3 = rows([0, 1, 2], range(KROW), (0, 3))
    bot2, bot1 = rows([67, 68, 69], range(KROW), (2, 1))
    side3, side1 = rows(range(W, W + SIDE), range(SIDE, KROW), (3, 1))

    cells = np.arange(SIDE * SIDE).reshape(SIDE, SIDE)
    bands = [
        cells[:W],
        np.rot90(cells[:, SIDE - W :], 1),
        np.rot90(cells[SIDE - W :], 2),
        np.rot90(cells[:, :W], 3),
    ]
    sels = []
    for s, band in enumerate(bands):
        sel = np.zeros((256, 192 if s in (0, 2) else 1024), np.float32)
        for w in range(W):
            for l in range(SIDE):
                i, j = divmod(int(band[w, l]), SIDE)
                if s == 0:
                    col = i * SIDE + j
                elif s == 2:
                    col = (i - (SIDE - W)) * SIDE + j
                elif s == 1:
                    col = i * 16 + j - 48
                else:
                    col = i * 16 + j
                st, a = where[w, l]
                sel[st * CELLS + a, col] = 1
        sels.append(sel)
    assemble = (top0, top3, bot2, bot1, side3, side1)
    return assemble, tuple(sels)


@functools.lru_cache(None)
def dft_tables():
    n = 2 * NFREQ
    theta = 2 * np.pi * (np.arange(NFREQ) + 0.5) / n

    def cs(pos):
        ang = theta[:, None] * np.asarray(pos, np.float64)[None, :]
        live = (np.asarray(pos) >= 0)[None, :]
        return np.cos(ang) * live, np.sin(ang) * live

    cols = [column_of(m) for m in range(KROW)]
    c, s = cs(cols)
    fwd_x = np.concatenate([c, -s, c - s], 0)
    inv_p = (2 / n) * np.concatenate([c + s, -c + s, -s], 0).T
    c, s = cs(np.arange(SIDE))
    inv_y = (2 / n) * np.concatenate([c + s, -c + s, -s], 0).T
    fwd_g = np.concatenate([c, -s, c - s, c + s], 0)
    taps = [0, 1, 2, 3, 4, 5, 6, -1]
    c, s = cs(taps)
    fwd_k = np.concatenate([c, s, c + s, c, -s, c - s], 0)
    inv_k = (2 / n) * np.concatenate([c + s, c - s, -s], 0).T
    hi = fwd_x.astype(jnp.bfloat16)
    lo = (fwd_x - hi.astype(np.float64)).astype(jnp.bfloat16)
    return (
        np.concatenate([hi, lo], 1),
        inv_y.astype(jnp.bfloat16),
        fwd_g.astype(jnp.bfloat16),
        inv_p.astype(jnp.bfloat16),
        fwd_k.astype(np.float32),
        inv_k.astype(np.float32),
    )


def dot(a, b):
    return jnp.dot(a, b, preferred_element_type=F32)


def dot_nt(a, b):
    return lax.dot_general(a, b, (((1,), (1,)), ((), ())), preferred_element_type=F32)


def dot_tn(a, b):
    return lax.dot_general(a, b, (((0,), (0,)), ((), ())), preferred_element_type=F32)


def dot_exact(a, b):
    return jnp.dot(a, b, preferred_element_type=F32, precision=lax.Precision.HIGHEST)


def peer(me, off, n):
    return lax.rem(me + off, n)


def greet(axes):
    barrier = pltpu.get_barrier_semaphore()
    total = 0
    for axis, n in axes:
        me = lax.axis_index(axis)
        for off in range(1, n):
            pl.semaphore_signal(
                barrier, inc=1, device_id={axis: peer(me, off, n)}, device_id_type=MESH
            )
            total += 1
    return barrier, total


def exchange(axis, n, src_of, dst, send, recv):
    me = lax.axis_index(axis)
    copies = []
    for off in range(1, n):
        to = peer(me, off, n)
        copy = pltpu.make_async_remote_copy(
            src_ref=src_of(to),
            dst_ref=dst(me),
            send_sem=send.at[off],
            recv_sem=recv.at[off],
            device_id={axis: to},
            device_id_type=MESH,
        )
        copy.start()
        copies.append(copy)
    return copies


def finish(copies):
    for copy in copies:
        copy.wait()


def halo_kernel(
    field, sel_n, sel_e, sel_s, sel_w, target, out, own, got, routed, back, s1, r1, s2, r2
):
    me = lax.axis_index("tile")
    barrier, total = greet((("tile", TILES),))
    shape = (TILES, CELLS, CH)
    own[0] = dot(sel_n[...], field[0:W].reshape(W * SIDE, CH)).astype(BF).reshape(shape)
    own[1] = dot(sel_e[...], field[:, 48:64].reshape(1024, CH)).astype(BF).reshape(shape)
    own[2] = dot(sel_s[...], field[SIDE - W :].reshape(W * SIDE, CH)).astype(BF).reshape(shape)
    own[3] = dot(sel_w[...], field[:, 0:16].reshape(1024, CH)).astype(BF).reshape(shape)
    pl.semaphore_wait(barrier, total)
    copies = exchange("tile", TILES, lambda to: own.at[:, to], lambda m: got.at[:, m], s1, r1)
    got[:, me] = own[:, me]
    columns = lax.broadcasted_iota(jnp.int32, (1024, 1024), 1)
    route = (columns == target[...]).astype(F32).astype(BF)
    finish(copies)
    moved = dot(route, got[...].reshape(1024, CH)).astype(BF)
    routed[...] = moved.reshape(4, TILES, CELLS, CH)
    copies = exchange("tile", TILES, lambda to: routed.at[:, to], lambda m: back.at[:, m], s2, r2)
    back[:, me] = routed[:, me]
    finish(copies)
    out[...] = back[...].reshape(4, 256, CH)


def halo(fields, target_col):
    _, sels = static_tables()
    sels = [jnp.asarray(s, BF) for s in sels]
    vm = pl.BlockSpec(memory_space=pltpu.VMEM)
    block = pltpu.VMEM((4, TILES, CELLS, CH), BF)
    sem = pltpu.SemaphoreType.DMA((TILES,))
    return pl.pallas_call(
        halo_kernel,
        out_shape=jax.ShapeDtypeStruct((4, 256, CH), BF),
        in_specs=[vm] * 6,
        out_specs=vm,
        scratch_shapes=[block, block, block, block, sem, sem, sem, sem],
        compiler_params=pltpu.CompilerParams(
            collective_id=0, has_side_effects=True, vmem_limit_bytes=40 * 2**20
        ),
        name="halo",
    )(fields, *sels, target_col)


def return_kernel(
    slots, target, wsrc, out, wout, got, routed, back, w1, w2, w2s, w3, s1, r1, s2, r2, ws1, wr1, ws2, wr2, ws3, wr3
):
    me = lax.axis_index("tile")
    md = lax.axis_index("dp")
    ndp = w2.shape[0]
    barrier, total = greet((("tile", TILES), ("dp", ndp)))
    pl.semaphore_wait(barrier, total)
    c1 = exchange("tile", TILES, lambda to: slots.at[:, to], lambda m: got.at[:, m], s1, r1)
    c2 = exchange("tile", TILES, lambda to: wsrc.at[to], lambda m: w1.at[m], ws1, wr1)
    got[:, me] = slots[:, me]
    w1[me] = wsrc[me]
    rows = lax.broadcasted_iota(jnp.int32, (1024, 1024), 0)
    route = (rows == target[...]).astype(F32).astype(BF)
    finish(c1)
    moved = dot(route, got[...].reshape(1024, CH)).astype(BF)
    routed[...] = moved.reshape(4, TILES, CELLS, CH)
    c1 = exchange("tile", TILES, lambda to: routed.at[:, to], lambda m: back.at[:, m], s2, r2)
    back[:, me] = routed[:, me]
    finish(c2)
    part = w1[0].astype(F32)
    for j in range(1, TILES):
        part = part + w1[j].astype(F32)
    w2s[...] = part
    c2 = exchange("dp", ndp, lambda to: w2s, lambda m: w2.at[m], ws2, wr2)
    w2[md] = part
    finish(c2)
    part = w2[0]
    for j in range(1, ndp):
        part = part + w2[j]
    w3[me] = part
    c2 = exchange("tile", TILES, lambda to: w3.at[me], lambda m: w3.at[m], ws3, wr3)
    finish(c1)
    out[...] = back[...].reshape(4, 256, CH)
    finish(c2)
    wout[...] = w3[...].reshape(WROWS, 128)


def send_back(slots, target_row, wsrc, ndp):
    vm = pl.BlockSpec(memory_space=pltpu.VMEM)
    block = pltpu.VMEM((4, TILES, CELLS, CH), BF)
    sem = pltpu.SemaphoreType.DMA((TILES,))
    sem_dp = pltpu.SemaphoreType.DMA((ndp,))
    return pl.pallas_call(
        return_kernel,
        out_shape=(
            jax.ShapeDtypeStruct((4, 256, CH), BF),
            jax.ShapeDtypeStruct((WROWS, 128), F32),
        ),
        in_specs=[vm] * 3,
        out_specs=(vm, vm),
        scratch_shapes=[
            block,
            block,
            block,
            pltpu.VMEM((TILES, WBLOCK, 128), BF),
            pltpu.VMEM((ndp, WBLOCK, 128), F32),
            pltpu.VMEM((WBLOCK, 128), F32),
            pltpu.VMEM((TILES, WBLOCK, 128), F32),
            sem,
            sem,
            sem,
            sem,
            sem,
            sem,
            sem_dp,
            sem_dp,
            sem,
            sem,
        ],
        compiler_params=pltpu.CompilerParams(
            collective_id=1, has_side_effects=True, vmem_limit_bytes=40 * 2**20
        ),
        name="send_back",
    )(slots, target_row, wsrc)


LANES = ((0, 128), (128, 64))


def block_kernel(
    fields,
    cot,
    hal,
    top0,
    top3,
    bot2,
    bot1,
    side3,
    side1,
    top0t,
    top3t,
    bot2t,
    bot1t,
    side3t,
    side1t,
    fwd_x,
    inv_y,
    fwd_g,
    inv_p,
    fwd_k,
    inv_k,
    kernel,
    conv_bias,
    gain,
    nbias,
    w_exp,
    b_exp,
    w_red,
    b_red,
    lscale,
    mixed,
    direct,
    slots,
    wout,
    xpad,
    x3,
    y3,
    g4,
    kpad,
    kf,
    m3,
    egrad,
    rgrad,
    psides,
    ptop,
    pbot,
):
    for u in range(7):
        kpad[0:7] = kernel[u]
        kpad[7:8] = jnp.zeros((1, CH), F32)
        kf[u] = dot_exact(fwd_k[...], kpad[...])
    xpad[W : W + SIDE, 0:SIDE] = fields[...]
    xpad[0:W] = (dot(top0[...], hal[0]) + dot(top3[...], hal[3])).astype(BF).reshape(W, KROW, CH)
    xpad[W + SIDE :] = (
        (dot(bot2[...], hal[2]) + dot(bot1[...], hal[1])).astype(BF).reshape(W, KROW, CH)
    )
    xpad[W : W + SIDE, SIDE:] = (
        (dot(side3[...], hal[3]) + dot(side1[...], hal[1])).astype(BF).reshape(SIDE, 16, CH)
    )

    def to_freq(r, _):
        x = xpad[r]
        x3[r] = dot(fwd_x[...], jnp.concatenate([x, x], axis=0))
        return 0

    lax.fori_loop(0, EXT, to_freq, 0, unroll=2)

    for l0, lw in LANES:
        for fb in range(5):
            rows = [slice(40 * t + 8 * fb, 40 * t + 8 * fb + 8) for t in range(3)]
            lanes = slice(l0, l0 + lw)
            kk = [[kf[u, rows[t], lanes] for t in range(3)] for u in range(7)]

            def conv(ib, _, rows=rows, lanes=lanes, kk=kk):
                i0 = ib * 4
                for t in range(3):
                    xs = [x3[i0 + r, rows[t], lanes] for r in range(10)]
                    for d in range(4):
                        acc = xs[d] * kk[0][t]
                        for u in range(1, 7):
                            acc = acc + xs[d + u] * kk[u][t]
                        y3[i0 + d, rows[t], lanes] = acc
                return 0

            lax.fori_loop(0, SIDE // 4, conv, 0)

    egrad[...] = jnp.zeros_like(egrad)
    rgrad[...] = jnp.zeros_like(rgrad)
    g4[0:6] = jnp.zeros((6, 4 * NFREQ, CH), F32)
    g4[6 + SIDE :] = jnp.zeros((6, 4 * NFREQ, CH), F32)
    step = 8
    n = step * SIDE

    def chunk(ic, _):
        i0 = pl.multiple_of(ic * step, step)
        conv_out = jnp.concatenate(
            [dot(inv_y[...], y3[i0 + d].astype(BF)) for d in range(step)], axis=0
        )
        conv_out = conv_out + conv_bias[...]
        shifted = conv_out - jnp.mean(conv_out, axis=-1, keepdims=True)
        inv_std = lax.rsqrt(jnp.mean(shifted * shifted, axis=-1, keepdims=True) + 1e-06)
        centred = shifted * inv_std
        normed = (centred * gain[...] + nbias[...]).astype(BF)
        pre = dot(normed, w_exp[...]) + b_exp[...]
        size = jnp.abs(pre)
        t = 1.0 / (1.0 + (0.3275911 * math.sqrt(0.5)) * size)
        dens = jnp.exp(-0.5 * pre * pre)
        poly = t * (
            0.127414796
            + t * (-0.142248368 + t * (0.7107068705 + t * (-0.7265760135 + t * 0.5307027145)))
        )
        tail = poly * dens
        phi = jnp.where(pre >= 0, 1.0 - tail, tail)
        act = (pre * phi).astype(BF)
        slope = phi + pre * (dens * 0.3989422804014327)
        cot_c = cot[pl.ds(i0, step)].reshape(n, CH).astype(F32)
        branch = dot(act, w_red[...]) + b_red[...]
        mix = fields[pl.ds(i0, step)].reshape(n, CH).astype(F32) + lscale[...] * branch
        mixed[pl.ds(i0, step)] = mix.astype(BF).reshape(step, SIDE, CH)
        bgrad = (lscale[...] * cot_c).astype(BF)
        pre_grad = (dot_nt(bgrad, w_red[...]) * slope).astype(BF)
        rgrad[...] += dot_tn(bgrad, act)
        egrad[...] += dot_tn(normed, pre_grad)
        ngrad = dot_nt(pre_grad, w_exp[...]) * gain[...]
        m1 = jnp.mean(ngrad, axis=-1, keepdims=True)
        m2 = jnp.mean(ngrad * centred, axis=-1, keepdims=True)
        cgrad = (inv_std * (ngrad - m1 - centred * m2)).astype(BF)
        for d in range(step):
            g4[6 + i0 + d] = dot(fwd_g[...], cgrad[d * SIDE : (d + 1) * SIDE])
        return 0

    lax.fori_loop(0, SIDE // step, chunk, 0)

    for l0, lw in LANES:
        for fb in range(5):
            rows = [slice(40 * t + 8 * fb, 40 * t + 8 * fb + 8) for t in range(4)]
            grow = (rows[0], rows[1], rows[3])
            lanes = slice(l0, l0 + lw)

            def kgrad(ib, accs, rows=rows, lanes=lanes, grow=grow):
                i0 = ib * 4
                accs = list(accs)
                for t in range(3):
                    xs = [x3[i0 + r, rows[t], lanes] for r in range(10)]
                    for d in range(4):
                        g = g4[6 + i0 + d, grow[t], lanes]
                        for u in range(7):
                            accs[7 * t + u] = accs[7 * t + u] + xs[d + u] * g
                return tuple(accs)

            zero = jnp.zeros((8, lw), F32)
            accs = lax.fori_loop(0, SIDE // 4, kgrad, (zero,) * 21)
            for t in range(3):
                for u in range(7):
                    m3[u, rows[t], lanes] = accs[7 * t + u]

            kk = [
                [kf[u, 120 + 40 * t + 8 * fb : 128 + 40 * t + 8 * fb, lanes] for t in range(3)]
                for u in range(7)
            ]

            def pconv(ib, _, rows=rows, lanes=lanes, kk=kk):
                p0 = ib * 5
                for t in range(3):
                    gs = [g4[p0 + r, rows[t], lanes] for r in range(11)]
                    for d in range(5):
                        acc = gs[d + 6] * kk[0][t]
                        for u in range(1, 7):
                            acc = acc + gs[d + 6 - u] * kk[u][t]
                        y3[p0 + d, rows[t], lanes] = acc
                return 0

            lax.fori_loop(0, EXT // 5, pconv, 0)

    for p in range(W):
        ptop[p] = dot(inv_p[...], y3[p].astype(BF)).astype(BF)
        pbot[p] = dot(inv_p[...], y3[W + SIDE + p].astype(BF)).astype(BF)

    def from_freq(i, _):
        back = dot(inv_p[...], y3[i + W].astype(BF))
        direct[i] = (cot[i].astype(F32) + back[0:SIDE]).astype(BF)
        psides[i] = back[SIDE:].astype(BF)
        return 0

    lax.fori_loop(0, SIDE, from_freq, 0, unroll=2)

    top = ptop[...].reshape(W * KROW, CH)
    bot = pbot[...].reshape(W * KROW, CH)
    sides = psides[...].reshape(SIDE * 16, CH)
    shape = (TILES, CELLS, CH)
    slots[0] = dot(top0t[...], top).astype(BF).reshape(shape)
    slots[1] = (dot(side1t[...], sides) + dot(bot1t[...], bot)).astype(BF).reshape(shape)
    slots[2] = dot(bot2t[...], bot).astype(BF).reshape(shape)
    slots[3] = (dot(side3t[...], sides) + dot(top3t[...], top)).astype(BF).reshape(shape)

    for g in range(3):
        lanes = slice(128 * g, 128 * g + 128)
        wout[192 * g : 192 * g + 192] = egrad[:, lanes].astype(BF)
        wout[576 + 192 * g : 768 + 192 * g] = rgrad[:, lanes].astype(BF)
    kg = jnp.concatenate([dot_exact(inv_k[...], m3[u]) for u in range(7)], axis=0)
    kg = jnp.concatenate([kg, jnp.zeros((8, CH), F32)], axis=0).astype(BF)
    wout[1152:1216] = kg[:, 0:128]
    wout[1216:1280] = jnp.concatenate([kg[:, 128:192], jnp.zeros((64, 64), BF)], axis=1)


def block(fields, cotangent, hal, params):
    assemble, _ = static_tables()
    mats = [jnp.asarray(a, BF) for a in assemble]
    mats_t = [jnp.asarray(a.T, BF) for a in assemble]
    tables = [jnp.asarray(t) for t in dft_tables()]
    vm = pl.BlockSpec(memory_space=pltpu.VMEM)
    args = [fields, cotangent, hal, *mats, *mats_t, *tables, *params]
    return pl.pallas_call(
        block_kernel,
        out_shape=(
            jax.ShapeDtypeStruct((SIDE, SIDE, CH), BF),
            jax.ShapeDtypeStruct((SIDE, SIDE, CH), BF),
            jax.ShapeDtypeStruct((4, TILES, CELLS, CH), BF),
            jax.ShapeDtypeStruct((WROWS, 128), BF),
        ),
        in_specs=[vm] * len(args),
        out_specs=(vm,) * 4,
        scratch_shapes=[
            pltpu.VMEM((EXT, KROW, CH), BF),
            pltpu.VMEM((EXT, 3 * NFREQ, CH), F32),
            pltpu.VMEM((EXT, 3 * NFREQ, CH), F32),
            pltpu.VMEM((SIDE + 12, 4 * NFREQ, CH), F32),
            pltpu.VMEM((8, CH), F32),
            pltpu.VMEM((7, 6 * NFREQ, CH), F32),
            pltpu.VMEM((7, 3 * NFREQ, CH), F32),
            pltpu.VMEM((CH, HID), F32),
            pltpu.VMEM((CH, HID), F32),
            pltpu.VMEM((SIDE, 16, CH), BF),
            pltpu.VMEM((W, KROW, CH), BF),
            pltpu.VMEM((W, KROW, CH), BF),
        ],
        compiler_params=pltpu.CompilerParams(vmem_limit_bytes=60 * 2**20),
        name="block",
    )(*args)


def last_kernel(scale, direct, bands, wsum, tn, te, ts, tw, out, kgrad, egrad, rgrad):
    north = dot(tn[...], bands[0]).reshape(W, SIDE, CH)
    south = dot(ts[...], bands[2]).reshape(W, SIDE, CH)
    east = dot(te[...], bands[1]).reshape(SIDE, 16, CH)
    west = dot(tw[...], bands[3]).reshape(SIDE, 16, CH)
    mid = slice(W, SIDE - W)
    out[mid, 16:48] = direct[mid, 16:48]
    out[mid, 0:16] = (direct[mid, 0:16].astype(F32) + west[mid]).astype(BF)
    out[mid, 48:64] = (direct[mid, 48:64].astype(F32) + east[mid]).astype(BF)
    zero = jnp.zeros((W, 32, CH), F32)
    for rows, add in ((slice(0, W), north), (slice(SIDE - W, SIDE), south)):
        more = jnp.concatenate([west[rows], zero, east[rows]], axis=1)
        out[rows] = (direct[rows].astype(F32) + add + more).astype(BF)
    for g in range(3):
        lanes = slice(128 * g, 128 * g + 128)
        egrad[:, lanes] = wsum[192 * g : 192 * g + 192] * scale
        rgrad[lanes, :] = wsum[576 + 192 * g : 768 + 192 * g].T * scale
    for u in range(7):
        kgrad[u, :, 0:128] = wsum[1152 + 8 * u : 1159 + 8 * u] * scale
        kgrad[u, :, 128:192] = wsum[1216 + 8 * u : 1223 + 8 * u, 0:64] * scale


def last(direct, bands, wsum, scale):
    _, sels = static_tables()
    sels_t = [jnp.asarray(s.T, BF) for s in sels]
    vm = pl.BlockSpec(memory_space=pltpu.VMEM)
    return pl.pallas_call(
        functools.partial(last_kernel, scale),
        out_shape=(
            jax.ShapeDtypeStruct((SIDE, SIDE, CH), BF),
            jax.ShapeDtypeStruct((7, 7, CH), F32),
            jax.ShapeDtypeStruct((CH, HID), F32),
            jax.ShapeDtypeStruct((HID, CH), F32),
        ),
        in_specs=[vm] * 7,
        out_specs=(vm,) * 4,
        compiler_params=pltpu.CompilerParams(vmem_limit_bytes=40 * 2**20),
        name="last",
    )(direct, bands, wsum, *sels_t)


def routing(neighbors, rotations):
    me = lax.axis_index("tile")
    offsets = jnp.array(OFFSETS, jnp.int32)[None, :]
    side = (rotations + offsets) % 4
    base = jnp.where(neighbors >= 0, side * 256 + neighbors * CELLS, -(1 << 20)).T
    right = jnp.where(me >= 7, 11, -(1 << 20))
    left = jnp.where(me <= 8, 0, -(1 << 20))
    corner_row = jnp.stack([right, left, right, left])[:, None]
    cell = jnp.arange(CELLS, dtype=jnp.int32)[None, None, :]
    edge = base[0:4][:, :, None] + cell
    corner = (base[4:8] + corner_row)[:, :, None]
    return jnp.where(cell < 12, edge, jnp.where(cell == 12, corner, -1)).astype(jnp.int32)


def on_device(
    fields,
    cotangent,
    kernel,
    conv_bias,
    norm_gain,
    norm_bias,
    w_expand,
    bias_expand,
    w_reduce,
    bias_reduce,
    layer_scale,
    neighbors,
    rotations,
):
    ndp = lax.axis_size("dp")
    field = fields.reshape(SIDE, SIDE, CH)
    cot = cotangent.reshape(SIDE, SIDE, CH)
    target = routing(neighbors, rotations)
    hal = halo(field, target.reshape(1024, 1))
    params = [
        kernel,
        conv_bias.reshape(1, CH),
        norm_gain.reshape(1, CH),
        norm_bias.reshape(1, CH),
        w_expand,
        bias_expand.reshape(1, HID),
        w_reduce,
        bias_reduce.reshape(1, CH),
        layer_scale.reshape(1, CH),
    ]
    mixed, direct, slots, wgrad = block(field, cot, hal, params)
    bands, wsum = send_back(
        slots, target.reshape(1, 1024), wgrad.reshape(TILES, WBLOCK, 128), ndp
    )
    scale = 1.0 / math.sqrt(ndp * TILES * SIDE * SIDE)
    input_grad, kgrad, egrad, rgrad = last(direct, bands, wsum, scale)
    return (
        mixed.reshape(fields.shape),
        input_grad.reshape(fields.shape),
        kgrad,
        egrad,
        rgrad,
    )


def solution(mesh):
    split = P("dp", "tile", None, None, None)
    return jax.shard_map(
        on_device,
        mesh=mesh,
        in_specs=(split, split) + (P(),) * 11,
        out_specs=(split, split, P(), P(), P()),
        check_vma=False,
    )
```

time: 529 us -> 133 us (0.25)
  other arithmetic: 227 us -> 1.02 us
  waiting for transfers between devices: 163 us -> 0 us
  Pallas kernels: 0 us -> 116 us
  blocking collectives: 64.9 us -> 0 us
  local copies, waits for them, and re-layouts: 38.2 us -> 14.1 us
  matrix products: 20.4 us -> 0 us
  between operations: 14.3 us -> 0.76 us
    pallas_call x0 -> x4, Pallas kernels: none -> 116 us  [the longest x1 52 us: block(): pl.pallas_call(block_kernel, out_shape=(jax.ShapeDtypeStruct((SIDE, SIDE,...]
    add x1 -> x0, other arithmetic: 110 us -> none  [block_batch(): padded_grad + kernel[row_off, col_off] * grown[:, low_row:low_row + exten...]
    reduce_scatter x1 -> x0, waiting for transfers between devices: 88.1 us -> none  [on_device(): lax.psum_scatter(operand.reshape(samples, all_tiles, 4, width, side, chan...]
    reduce_sum x6 -> x0, other arithmetic: 75.2 us -> none  [the longest x3 36.8 us: block_batch(): kernel_terms.append(jnp.sum(window * conv_grad, axis=(0, 1, 2)))]
    psum x1 -> x0, blocking collectives: 64.9 us -> none  [on_device(): totals = lax.psum((grads[0], grads[1], grads[2]), ('dp', 'tile'))]
    all_gather x1 -> x0, waiting for transfers between devices: 61.8 us -> none  [on_device(): lax.all_gather(for_sending(band_set), 'tile', axis=1, tiled=True)]
    convert_element_type x6 -> x0, other arithmetic: 24.9 us -> none  [the longest x1 8.21 us: on_device(): operand.reshape(samples, all_tiles, 4, width, side, channels)]
    dot_general x6 -> x0, matrix products: 20.4 us -> none  [the longest x1 4.83 us: block_batch(): jnp.dot(activated, w_reduce, preferred_element_type=jnp.float32)]
  transfers between devices with their start and end apart: 3 -> 0, of which waited for: 3 -> 0; matrix products, arithmetic and copies ran while one was open for 14% -> 0% of each run, Pallas kernels for 0% -> 0%
where the time goes in v1:
time: 133 us; the launch traced here: 132 us
  Pallas kernels  116 us (87%)
  local copies, waits for them, and re-layouts  14.1 us (11%)
    pallas_call x1, Pallas kernels, block(): pl.pallas_call(block_kernel, out_shape=(jax.ShapeDtypeStruct((SIDE, SIDE,...  52 us
    pallas_call x1, Pallas kernels, send_back(): pl.pallas_call(return_kernel, out_shape=(jax.ShapeDtypeStruct((4, 256, CH...  37 us
    pallas_call x1, Pallas kernels, halo(): pl.pallas_call(halo_kernel, out_shape=jax.ShapeDtypeStruct((4, 256, CH),...  25.4 us
    unnamed x28, local copies, waits for them, and re-layouts  12.5 us

profile of v1, /device:TPU:1, one launch (start us, length us, event | category | flops | bytes accessed | tf_op | source)
XLA Modules:
  0.0 132.2 jit_solution(4316110328999169483)
XLA Ops:
  0.6 0.1 pad_add_fusion
  0.7 1.2 reshape.180.b_exp
  2.0 0.8 fusion.4
  2.8 0.1 fusion.5
  2.8 0.1 select_select_fusion
  2.9 0.1 select_n.69.target
  3.0 1.7 %copy.48.w_red = bf16[384,192]{1,0:T(8,128)(2,1)} copy(bf16[384,192]{0,1:T(8,128)(2,1)} %param.48) | data formatting | bytes 294912 | tf_op args[8]
  4.7 0.3 select_n.70.target
  5.0 0.0 copy-start
  5.0 1.6 %copy-done = bf16[1,1,64,64,192]{4,3,2,1,0:T(8,128)(2,1)S(1)} copy-done((bf16[1,1,64,64,192]{4,3,2,1,0:T(8,128)(2,1)S(1)}, bf16[1,1,64,64,192]{4,3,2,1,0:T(8,128)(2,1)}, u32[]{:S(2)}) %copy-start) | copy-done | bytes 1572888
  6.6 1.0 copy-done.5
  7.7 1.0 copy-done.6
  8.7 0.9 copy-done.9
  9.6 0.9 copy-done.10
  10.5 25.4 %halo.1.hal = bf16[4,256,192]{2,1,0:T(8,128)(2,1)S(1)} custom-call(bf16[64,64,192]{2,1,0:T(8,128)(2,1)S(1)} %bitcast.15, bf16[256,192]{1,0:T(8,128)(2,1)S(1)} %copy-done.10, bf16[256,1024]{1,0:T(8,128)(2,1)S(1)} %copy-done.6, bf16[256,192]{1,0:T(8,128)(2,1)S(1)} %copy-done.9, bf16[256,1024]{1,0:T(8,128)(2,1)S(1)} %copy-done.5, s32[1024,1]{1,0:T(8,128)S(1)} %select_n.70.target), custom_call_target="tpu_custom_call" | custom-call | tf_op jit(solution)/shard_map/halo/pallas_call | solution.py:252
  35.9 0.8 copy-done.1
  36.7 52.0 %block.1 = (bf16[64,64,192]{2,1,0:T(8,128)(2,1)}, bf16[64,64,192]{2,1,0:T(8,128)(2,1)}, bf16[4,16,16,192]{3,2,1,0:T(8,128)(2,1)}, bf16[1280,128]{1,0:T(8,128)(2,1)}) custom-call(bf16[64,64,192]{2,1,0:T(8,128)(2,1)} %bitcast.14, bf16[64,64,192]{2,1,0:T(8,128)(2,1)} %bitcast.17, bf16[4,256,192]{2,1,0:T(8,128)(2,1)} %copy-done.1, ...), custom_call_target="tpu_custom_call" | custom-call | tf_op jit(solution)/shard_map/block/pallas_call | solution.py:558
  88.7 1.0 copy-done.7
  89.7 1.0 copy-done.8
  90.7 37.0 %send_back.1 = (bf16[4,256,192]{2,1,0:T(8,128)(2,1)S(1)}, f32[1280,128]{1,0:T(8,128)S(1)}) custom-call(bf16[4,16,16,192]{3,2,1,0:T(8,128)(2,1)S(1)} %copy-done.7, s32[1,1024]{1,0:T(1,128)S(1)} %select_n.69.target, bf16[16,80,128]{2,1,0:T(8,128)(2,1)S(1)} %bitcast.16), custom_call_target="tpu_custom_call" | custom-call | tf_op jit(solution)/shard_map/send_back/pallas_call | solution.py:308
  127.8 0.0 copy-start.2
  127.8 1.6 %copy-done.2 = bf16[64,64,192]{2,1,0:T(8,128)(2,1)S(1)} copy-done((bf16[64,64,192]{2,1,0:T(8,128)(2,1)S(1)}, bf16[64,64,192]{2,1,0:T(8,128)(2,1)}, u32[]{:S(2)}) %copy-start.2) | copy-done | bytes 1572888
  129.4 1.9 %last.1 = (bf16[64,64,192]{2,1,0:T(8,128)(2,1)}, f32[7,7,192]{2,1,0:T(8,128)}, f32[192,384]{1,0:T(8,128)}, f32[384,192]{1,0:T(8,128)S(1)}) custom-call(bf16[64,64,192]{2,1,0:T(8,128)(2,1)S(1)} %copy-done.2, bf16[4,256,192]{2,1,0:T(8,128)(2,1)S(1)} %get-tuple-element.19.bands, f32[1280,128]{1,0:T(8,128)S(1)} %get-tuple-element.20.wsum, ...), custom_call_target="tpu_custom_call" | custom-call | tf_op jit(solution)/shard_map/last/pallas_call | solution.py:613
  131.3 0.9 copy.49
  (16 shorter events, 0.0 us)
Async XLA Ops:
  5.0 1.6 %copy-start = (bf16[1,1,64,64,192]{4,3,2,1,0:T(8,128)(2,1)S(1)}, bf16[1,1,64,64,192]{4,3,2,1,0:T(8,128)(2,1)}, u32[]{:S(2)}) copy-start(bf16[1,1,64,64,192]{4,3,2,1,0:T(8,128)(2,1)} %param.40) | copy-start | bytes 4718596
  6.6 1.0 copy-start.5
  7.7 1.0 copy-start.6
  8.7 0.9 copy-start.9
  9.6 0.9 copy-start.10
  35.9 0.8 copy-start.1
  36.7 91.0 %copy-start.3 = (bf16[1024,256]{1,0:T(8,128)(2,1)S(1)}, bf16[1024,256]{1,0:T(8,128)(2,1)}, u32[]{:S(2)}) copy-start(bf16[1024,256]{1,0:T(8,128)(2,1)} %constant.117.clone.tw) | copy-start | bytes 1572868
  36.7 91.0 %copy-start.4 = (bf16[1024,256]{1,0:T(8,128)(2,1)S(1)}, bf16[1024,256]{1,0:T(8,128)(2,1)}, u32[]{:S(2)}) copy-start(bf16[1024,256]{1,0:T(8,128)(2,1)} %constant.115.clone.te) | copy-start | bytes 1572868
  36.7 91.1 %copy-start.11 = (bf16[192,256]{1,0:T(8,128)(2,1)S(1)}, bf16[192,256]{1,0:T(8,128)(2,1)}, u32[]{:S(2)}) copy-start(bf16[192,256]{1,0:T(8,128)(2,1)} %constant.116.clone.ts) | copy-start | bytes 294916
  36.7 91.1 %copy-start.12 = (bf16[192,256]{1,0:T(8,128)(2,1)S(1)}, bf16[192,256]{1,0:T(8,128)(2,1)}, u32[]{:S(2)}) copy-start(bf16[192,256]{1,0:T(8,128)(2,1)} %constant.114.clone.tn) | copy-start | bytes 294916
  88.7 1.0 copy-start.7
  89.7 1.0 copy-start.8
  127.8 1.6 %copy-start.2 = (bf16[64,64,192]{2,1,0:T(8,128)(2,1)S(1)}, bf16[64,64,192]{2,1,0:T(8,128)(2,1)}, u32[]{:S(2)}) copy-start(bf16[64,64,192]{2,1,0:T(8,128)(2,1)} %get-tuple-element.16.direct) | copy-start | bytes 4718596

commit v2 on v1

v2 whole, which is shorter than its diff:
```python
import functools
import math

import jax
import jax.numpy as jnp
import numpy as np
from jax import lax
from jax.experimental import pallas as pl
from jax.experimental.pallas import tpu as pltpu
from jax.sharding import PartitionSpec as P

OFFSETS = (2, 3, 0, 1, 2, 0, 0, 2)
SIDE = 64
W = 3
CH = 192
HID = 384
TILES = 16
CELLS = 16
NFREQ = 40
KROW = 80
EXT = SIDE + 2 * W
BF = jnp.bfloat16
F32 = jnp.float32
MESH = pl.DeviceIdType.MESH
WROWS = 1280
WBLOCK = 16
INDEX = ("top0", "top3", "bot2", "bot1", "side3", "side1", "north", "east", "south", "west")


def stripe_table():
    where = np.zeros((W, SIDE, 2), np.int64)
    used = {i: set() for i in range(16)}
    rest = []
    for w in range(W):
        for l in range(SIDE):
            if l < W:
                spot = (w * W + l, 0)
            elif l >= SIDE - W:
                spot = (7 + w * W + l - (SIDE - W), 11)
            else:
                rest.append((w, l))
                continue
            where[w, l] = spot
            used[spot[0]].add(spot[1])
    free = [(i, a) for i in range(16) for a in range(12) if a not in used[i]]
    for (w, l), spot in zip(rest, free):
        where[w, l] = spot
    return where


def np_pad(field, picked):
    north = np.rot90(picked[0], 2)
    east = np.rot90(picked[1], 1)
    south = picked[2]
    west = np.rot90(picked[3], 3)
    ne = np.rot90(picked[4], 2)[:, :W]
    se = picked[5][:, :W]
    sw = picked[6][:, SIDE - W :]
    nw = np.rot90(picked[7], 2)[:, SIDE - W :]
    return np.concatenate(
        [
            np.concatenate([nw, north, ne], 1),
            np.concatenate([west, field, east], 1),
            np.concatenate([sw, south, se], 1),
        ],
        0,
    )


def column_of(m):
    if m < SIDE:
        return m + W
    if m < SIDE + W:
        return m - SIDE
    if m < SIDE + 2 * W:
        return m
    return -1


@functools.lru_cache(None)
def static_tables():
    where = stripe_table()
    codes = np.arange(8 * W * SIDE).reshape(8, W, SIDE)
    padded = np_pad(np.full((SIDE, SIDE), -1), codes)

    def spot(code):
        k, w, l = np.unravel_index(code, (8, W, SIDE))
        i, a = where[w, l]
        return (k, i * CELLS + a) if k < 4 else (k - 4, i * CELLS + 12)

    index = {name: np.full(256, -1, np.int64) for name in INDEX}

    def places(p_list, m_list, names):
        for ip, p in enumerate(p_list):
            for im, m in enumerate(m_list):
                q = column_of(m)
                if q < 0 or padded[p, q] < 0:
                    continue
                k, row = spot(padded[p, q])
                index[names[k]][row] = ip * len(m_list) + im

    places([0, 1, 2], range(KROW), {0: "top0", 3: "top3"})
    places([67, 68, 69], range(KROW), {2: "bot2", 1: "bot1"})
    places(range(W, W + SIDE), range(SIDE, KROW), {3: "side3", 1: "side1"})

    cells = np.arange(SIDE * SIDE).reshape(SIDE, SIDE)
    bands = {
        "north": (cells[:W], SIDE, 0, 0),
        "east": (np.rot90(cells[:, SIDE - W :], 1), 16, 0, 48),
        "south": (np.rot90(cells[SIDE - W :], 2), SIDE, SIDE - W, 0),
        "west": (np.rot90(cells[:, :W], 3), 16, 0, 0),
    }
    for name, (band, pitch, row0, col0) in bands.items():
        for w in range(W):
            for l in range(SIDE):
                i, j = divmod(int(band[w, l]), SIDE)
                st, a = where[w, l]
                index[name][st * CELLS + a] = (i - row0) * pitch + j - col0
    table = np.stack([index[name] for name in INDEX]).astype(np.int32)
    by_row = np.full((16, 256), -1, np.int32)
    by_row[: len(INDEX)] = table
    by_col = np.full((256, 128), -1, np.int32)
    by_col[:, : len(INDEX)] = table.T
    return by_row, by_col


def spread(by_row, name, n):
    k = INDEX.index(name)
    place = lax.broadcasted_iota(jnp.int32, (n, 256), 0)
    return (place == by_row[k : k + 1]).astype(F32).astype(BF)


def gather(by_col, name, n):
    k = INDEX.index(name)
    place = lax.broadcasted_iota(jnp.int32, (256, n), 1)
    return (place == by_col[:, k : k + 1]).astype(F32).astype(BF)


@functools.lru_cache(None)
def dft_tables():
    n = 2 * NFREQ
    theta = 2 * np.pi * (np.arange(NFREQ) + 0.5) / n

    def cs(pos):
        ang = theta[:, None] * np.asarray(pos, np.float64)[None, :]
        live = (np.asarray(pos) >= 0)[None, :]
        return np.cos(ang) * live, np.sin(ang) * live

    def inverse(c, s):
        both = np.stack([c.reshape(5, 8, -1), -s.reshape(5, 8, -1)], 1)
        return (2 / n) * both.reshape(2 * NFREQ, -1).T

    cols = [column_of(m) for m in range(KROW)]
    c, s = cs(cols)
    fwd_x = np.concatenate([c, -s, c - s], 0)
    inv_p = inverse(c, s)
    c, s = cs(np.arange(SIDE))
    inv_y = inverse(c, s)
    fwd_g = np.concatenate([c, -s, c - s, c + s], 0)
    taps = [0, 1, 2, 3, 4, 5, 6, -1]
    c, s = cs(taps)
    fwd_k = np.concatenate([c, s, c + s, c, -s, c - s], 0)
    inv_k = (2 / n) * np.concatenate([c + s, c - s, -s], 0).T
    return (
        fwd_x.astype(jnp.bfloat16),
        inv_y.astype(jnp.bfloat16),
        fwd_g.astype(jnp.bfloat16),
        inv_p.astype(jnp.bfloat16),
        fwd_k.astype(np.float32),
        inv_k.astype(np.float32),
    )


def dot(a, b):
    return jnp.dot(a, b, preferred_element_type=F32)


def dot_nt(a, b):
    return lax.dot_general(a, b, (((1,), (1,)), ((), ())), preferred_element_type=F32)


def dot_tn(a, b):
    return lax.dot_general(a, b, (((0,), (0,)), ((), ())), preferred_element_type=F32)


def dot_exact(a, b):
    return jnp.dot(a, b, preferred_element_type=F32, precision=lax.Precision.HIGHEST)


def peer(me, off, n):
    return lax.rem(me + off, n)


def greet(axes):
    barrier = pltpu.get_barrier_semaphore()
    total = 0
    for axis, n in axes:
        me = lax.axis_index(axis)
        for off in range(1, n):
            pl.semaphore_signal(
                barrier, inc=1, device_id={axis: peer(me, off, n)}, device_id_type=MESH
            )
            total += 1
    return barrier, total


def exchange(axis, n, src_of, dst, send, recv):
    me = lax.axis_index(axis)
    copies = []
    for off in range(1, n):
        to = peer(me, off, n)
        copy = pltpu.make_async_remote_copy(
            src_ref=src_of(to),
            dst_ref=dst(me),
            send_sem=send.at[off],
            recv_sem=recv.at[off],
            device_id={axis: to},
            device_id_type=MESH,
        )
        copy.start()
        copies.append(copy)
    return copies


def finish(copies):
    for copy in copies:
        copy.wait()


PACKED = (6, TILES, CELLS, 128)


def pack(ref, value):
    ref[0:4] = value[..., 0:128]
    ref[4:6] = jnp.concatenate([value[0:2, :, :, 128:CH], value[2:4, :, :, 128:CH]], axis=-1)


def unpack(ref):
    low = ref[0:4].reshape(1024, 128)
    pair = ref[4:6].reshape(512, 128)
    high = jnp.concatenate([pair[:, 0:64], pair[:, 64:128]], axis=0)
    return jnp.concatenate([low, high], axis=-1)


def halo_kernel(field, by_col, target, out, own, got, routed, back, s1, r1, s2, r2):
    me = lax.axis_index("tile")
    barrier, total = greet((("tile", TILES),))
    bands = jnp.concatenate(
        [
            dot(gather(by_col, "north", W * SIDE), field[0:W].reshape(W * SIDE, CH)),
            dot(gather(by_col, "east", 1024), field[:, 48:64].reshape(1024, CH)),
            dot(gather(by_col, "south", W * SIDE), field[SIDE - W :].reshape(W * SIDE, CH)),
            dot(gather(by_col, "west", 1024), field[:, 0:16].reshape(1024, CH)),
        ],
        axis=0,
    )
    pack(own, bands.astype(BF).reshape(4, TILES, CELLS, CH))
    pl.semaphore_wait(barrier, total)
    copies = exchange("tile", TILES, lambda to: own.at[:, to], lambda m: got.at[:, m], s1, r1)
    got[:, me] = own[:, me]
    columns = lax.broadcasted_iota(jnp.int32, (1024, 1024), 1)
    route = (columns == target[...]).astype(F32).astype(BF)
    finish(copies)
    pack(routed, dot(route, unpack(got)).astype(BF).reshape(4, TILES, CELLS, CH))
    copies = exchange("tile", TILES, lambda to: routed.at[:, to], lambda m: back.at[:, m], s2, r2)
    back[:, me] = routed[:, me]
    finish(copies)
    out[...] = unpack(back).reshape(4, 256, CH)


def halo(fields, target_col):
    _, by_col = static_tables()
    vm = pl.BlockSpec(memory_space=pltpu.VMEM)
    block = pltpu.VMEM(PACKED, BF)
    sem = pltpu.SemaphoreType.DMA((TILES,))
    return pl.pallas_call(
        halo_kernel,
        out_shape=jax.ShapeDtypeStruct((4, 256, CH), BF),
        in_specs=[vm] * 3,
        out_specs=vm,
        scratch_shapes=[block, block, block, block, sem, sem, sem, sem],
        compiler_params=pltpu.CompilerParams(
            collective_id=0, has_side_effects=True, vmem_limit_bytes=24 * 2**20
        ),
        name="halo",
    )(fields, jnp.asarray(by_col), target_col)


def return_kernel(
    slots, target, wsrc, out, wout, got, routed, back, wa, pa, wb, pc, wc, wd, *sems
):
    s1, r1, s2, r2, sa, ra, sb, rb, sc, rc, sd, rd = sems
    me = lax.axis_index("tile")
    md = lax.axis_index("dp")
    ndp = wa.shape[0]
    owners = pa.shape[0]
    barrier, total = greet((("tile", TILES), ("dp", ndp)))
    pl.semaphore_wait(barrier, total)
    ca = exchange("dp", ndp, lambda to: wsrc.at[to], lambda m: wa.at[m], sa, ra)
    c1 = exchange("tile", TILES, lambda to: slots.at[:, to], lambda m: got.at[:, m], s1, r1)
    got[:, me] = slots[:, me]
    wa[md] = wsrc[md]
    rows = lax.broadcasted_iota(jnp.int32, (1024, 1024), 0)
    route = (rows == target[...]).astype(F32).astype(BF)

    finish(ca)
    part = wa[0].astype(F32)
    for j in range(1, ndp):
        part = part + wa[j].astype(F32)
    pa[...] = part.reshape(owners, WBLOCK, 128)

    def share(off, src, dst, send, recv):
        to = peer(me, off, TILES)
        return pltpu.make_async_remote_copy(
            src_ref=src,
            dst_ref=dst,
            send_sem=send.at[off],
            recv_sem=recv.at[off],
            device_id={"tile": to},
            device_id_type=MESH,
        )

    def to_owner(off):
        to = peer(me, off, TILES)
        return to, share(off, pa.at[lax.rem(to, owners)], wb.at[me], sb, rb)

    for off in range(1, TILES):
        to, copy = to_owner(off)
        pl.when(to < owners)(copy.start)

    @pl.when(me < owners)
    def _():
        wb[me] = pa[lax.rem(me, owners)]

    finish(c1)
    pack(routed, dot(route, unpack(got)).astype(BF).reshape(4, TILES, CELLS, CH))
    c2 = exchange("tile", TILES, lambda to: routed.at[:, to], lambda m: back.at[:, m], s2, r2)
    back[:, me] = routed[:, me]

    for off in range(1, TILES):
        to, copy = to_owner(off)
        pl.when(to < owners)(copy.wait_send)
        pl.when(me < owners)(copy.wait_recv)

    mine = lax.rem(me, owners)

    @pl.when(me < owners)
    def _():
        total = wb[0]
        for j in range(1, TILES):
            total = total + wb[j]
        pc[...] = total.astype(BF)
        wc[mine] = total.astype(BF)
        for off in range(1, TILES):
            share(off, pc, wc.at[mine], sc, rc).start()

    for off in range(1, TILES):
        copy = share(off, pc, wc.at[mine], sc, rc)
        pl.when(me < owners)(copy.wait_send)
        pl.when(peer(me, TILES - off, TILES) < owners)(copy.wait_recv)

    block = wc[...].reshape(owners * WBLOCK, 128)
    pd = wa.at[0]
    pd[...] = block
    cd = exchange("dp", ndp, lambda to: pd, lambda m: wd.at[m], sd, rd)
    wd[md] = block
    finish(c2)
    out[...] = unpack(back).reshape(4, 256, CH)
    finish(cd)
    wout[...] = wd[...].reshape(WROWS, 128)


def send_back(slots, target_row, wsrc, ndp):
    vm = pl.BlockSpec(memory_space=pltpu.VMEM)
    block = pltpu.VMEM(PACKED, BF)
    sem = pltpu.SemaphoreType.DMA((TILES,))
    sem_dp = pltpu.SemaphoreType.DMA((ndp,))
    dp_rows = WROWS // ndp
    owners = dp_rows // WBLOCK
    return pl.pallas_call(
        return_kernel,
        out_shape=(
            jax.ShapeDtypeStruct((4, 256, CH), BF),
            jax.ShapeDtypeStruct((WROWS, 128), BF),
        ),
        in_specs=[vm] * 3,
        out_specs=(vm, vm),
        scratch_shapes=[
            block,
            block,
            block,
            pltpu.VMEM((ndp, dp_rows, 128), BF),
            pltpu.VMEM((owners, WBLOCK, 128), F32),
            pltpu.VMEM((TILES, WBLOCK, 128), F32),
            pltpu.VMEM((WBLOCK, 128), BF),
            pltpu.VMEM((owners, WBLOCK, 128), BF),
            pltpu.VMEM((ndp, dp_rows, 128), BF),
        ]
        + [sem] * 4
        + [sem_dp] * 2
        + [sem] * 4
        + [sem_dp] * 2,
        compiler_params=pltpu.CompilerParams(
            collective_id=1, has_side_effects=True, vmem_limit_bytes=24 * 2**20
        ),
        name="send_back",
    )(slots, target_row, wsrc)


LANES = ((0, 128), (128, 64))


def taps(xs, ks):
    acc = xs[0] * ks[0]
    for x, k in zip(xs[1:], ks[1:]):
        acc = acc + x * k
    return acc


def real_imag(a, b, c):
    return jnp.concatenate([a - b, c - a - b], axis=0).astype(BF)


def block_kernel(
    fields,
    cot,
    hal,
    by_row,
    by_col,
    fwd_x,
    inv_y,
    fwd_g,
    inv_p,
    fwd_k,
    inv_k,
    kernel,
    conv_bias,
    gain,
    nbias,
    w_exp,
    b_exp,
    w_red,
    b_red,
    lscale,
    mixed,
    direct,
    slots,
    wout,
    xpad,
    x3,
    y2,
    g4,
    kpad,
    kf,
    m3,
    egrad,
    rgrad,
    psides,
    ptop,
    pbot,
):
    conv_bias, gain, nbias, b_exp, b_red, lscale = (
        ref[...].reshape(1, -1) for ref in (conv_bias, gain, nbias, b_exp, b_red, lscale)
    )
    for u in range(7):
        kpad[0:7] = kernel[u]
        kpad[7:8] = jnp.zeros((1, CH), F32)
        kf[u] = dot_exact(fwd_k[...], kpad[...])
    xpad[W : W + SIDE, 0:SIDE] = fields[...]

    def put(n, *parts):
        return sum(dot(spread(by_row, name, n), hal[k]) for name, k in parts).astype(BF)

    xpad[0:W] = put(W * KROW, ("top0", 0), ("top3", 3)).reshape(W, KROW, CH)
    xpad[W + SIDE :] = put(W * KROW, ("bot2", 2), ("bot1", 1)).reshape(W, KROW, CH)
    xpad[W : W + SIDE, SIDE:] = put(SIDE * 16, ("side3", 3), ("side1", 1)).reshape(SIDE, 16, CH)

    def to_freq(r, _):
        x3[r] = dot(fwd_x[...], xpad[r])
        return 0

    lax.fori_loop(0, EXT, to_freq, 0, unroll=14)

    for l0, lw in LANES:
        for fb in range(5):
            rows = [slice(40 * t + 8 * fb, 40 * t + 8 * fb + 8) for t in range(3)]
            lanes = slice(l0, l0 + lw)
            kk = [[kf[u, rows[t], lanes] for t in range(3)] for u in range(7)]

            def conv(ib, _, fb=fb, rows=rows, lanes=lanes, kk=kk):
                i0 = ib * 4
                prods = []
                for t in range(3):
                    xs = [x3[i0 + r, rows[t], lanes] for r in range(10)]
                    prods.append([taps(xs[d : d + 7], [k[t] for k in kk]) for d in range(4)])
                for d in range(4):
                    y2[i0 + d, 16 * fb : 16 * fb + 16, lanes] = real_imag(*(p[d] for p in prods))
                return 0

            lax.fori_loop(0, SIDE // 4, conv, 0, unroll=2)

    egrad[...] = jnp.zeros_like(egrad)
    rgrad[...] = jnp.zeros_like(rgrad)
    g4[0:6] = jnp.zeros((6, 4 * NFREQ, CH), F32)
    g4[6 + SIDE :] = jnp.zeros((6, 4 * NFREQ, CH), F32)
    step = 16
    n = step * SIDE

    def chunk(ic, _):
        i0 = pl.multiple_of(ic * step, step)
        conv_out = jnp.concatenate(
            [dot(inv_y[...], y2[i0 + d]) for d in range(step)], axis=0
        )
        conv_out = conv_out + conv_bias
        shifted = conv_out - jnp.mean(conv_out, axis=-1, keepdims=True)
        inv_std = lax.rsqrt(jnp.mean(shifted * shifted, axis=-1, keepdims=True) + 1e-06)
        centred = shifted * inv_std
        normed = (centred * gain + nbias).astype(BF)
        pre = dot(normed, w_exp[...]) + b_exp
        size = jnp.abs(pre)
        t = 1.0 / (1.0 + (0.3275911 * math.sqrt(0.5)) * size)
        dens = jnp.exp(-0.5 * pre * pre)
        poly = t * (
            0.127414796
            + t * (-0.142248368 + t * (0.7107068705 + t * (-0.7265760135 + t * 0.5307027145)))
        )
        tail = poly * dens
        phi = jnp.where(pre >= 0, 1.0 - tail, tail)
        act = (pre * phi).astype(BF)
        slope = phi + pre * (dens * 0.3989422804014327)
        cot_c = cot[pl.ds(i0, step)].reshape(n, CH).astype(F32)
        branch = dot_nt(act, w_red[...]) + b_red
        mix = fields[pl.ds(i0, step)].reshape(n, CH).astype(F32) + lscale * branch
        mixed[pl.ds(i0, step)] = mix.astype(BF).reshape(step, SIDE, CH)
        bgrad = (lscale * cot_c).astype(BF)
        pre_grad = (dot(bgrad, w_red[...]) * slope).astype(BF)
        rgrad[...] += dot_tn(bgrad, act)
        egrad[...] += dot_tn(normed, pre_grad)
        ngrad = dot_nt(pre_grad, w_exp[...]) * gain
        m1 = jnp.mean(ngrad, axis=-1, keepdims=True)
        m2 = jnp.mean(ngrad * centred, axis=-1, keepdims=True)
        cgrad = (inv_std * (ngrad - m1 - centred * m2)).astype(BF)
        for d in range(step):
            g4[6 + i0 + d] = dot(fwd_g[...], cgrad[d * SIDE : (d + 1) * SIDE])
        return 0

    lax.fori_loop(0, SIDE // step, chunk, 0)

    for l0, lw in LANES:
        for fb in range(5):
            rows = [slice(40 * t + 8 * fb, 40 * t + 8 * fb + 8) for t in range(4)]
            grow = (rows[0], rows[1], rows[3])
            lanes = slice(l0, l0 + lw)

            def kgrad(ib, accs, rows=rows, lanes=lanes, grow=grow):
                i0 = ib * 4
                accs = list(accs)
                for t in range(3):
                    xs = [x3[i0 + r, rows[t], lanes] for r in range(10)]
                    for d in range(4):
                        g = g4[6 + i0 + d, grow[t], lanes]
                        for u in range(7):
                            accs[7 * t + u] = accs[7 * t + u] + xs[d + u] * g
                return tuple(accs)

            zero = jnp.zeros((8, lw), F32)
            accs = lax.fori_loop(0, SIDE // 4, kgrad, (zero,) * 21, unroll=2)
            for t in range(3):
                for u in range(7):
                    m3[u, rows[t], lanes] = accs[7 * t + u]

            kk = [
                [kf[u, 120 + 40 * t + 8 * fb : 128 + 40 * t + 8 * fb, lanes] for t in range(3)]
                for u in range(7)
            ]

            def pconv(ib, _, fb=fb, rows=rows, lanes=lanes, kk=kk):
                p0 = ib * 5
                prods = []
                for t in range(3):
                    gs = [g4[p0 + r, rows[t], lanes] for r in range(11)]
                    back = [k[t] for k in kk][::-1]
                    prods.append([taps(gs[d : d + 7], back) for d in range(5)])
                for d in range(5):
                    y2[p0 + d, 16 * fb : 16 * fb + 16, lanes] = real_imag(*(p[d] for p in prods))
                return 0

            lax.fori_loop(0, EXT // 5, pconv, 0, unroll=2)

    for p in range(W):
        ptop[p] = dot(inv_p[...], y2[p]).astype(BF)
        pbot[p] = dot(inv_p[...], y2[W + SIDE + p]).astype(BF)

    def from_freq(i, _):
        back = dot(inv_p[...], y2[i + W])
        direct[i] = (cot[i].astype(F32) + back[0:SIDE]).astype(BF)
        psides[i] = back[SIDE:].astype(BF)
        return 0

    lax.fori_loop(0, SIDE, from_freq, 0, unroll=8)

    top = ptop[...].reshape(W * KROW, CH)
    bot = pbot[...].reshape(W * KROW, CH)
    sides = psides[...].reshape(SIDE * 16, CH)


    def take(*parts):
        total = sum(dot(gather(by_col, name, part.shape[0]), part) for name, part in parts)
        return total.astype(BF).reshape(1, TILES, CELLS, CH)

    taken = [
        take(("top0", top)),
        take(("side1", sides), ("bot1", bot)),
        take(("bot2", bot)),
        take(("side3", sides), ("top3", top)),
    ]
    pack(slots, jnp.concatenate(taken, axis=0))

    for g in range(3):
        lanes = slice(128 * g, 128 * g + 128)
        wout[192 * g : 192 * g + 192] = egrad[:, lanes].astype(BF)
        wout[576 + 192 * g : 768 + 192 * g] = rgrad[:, lanes].astype(BF)
    kg = jnp.concatenate([dot_exact(inv_k[...], m3[u]) for u in range(7)], axis=0)
    kg = jnp.concatenate([kg, jnp.zeros((8, CH), F32)], axis=0).astype(BF)
    wout[1152:1216] = kg[:, 0:128]
    wout[1216:1280] = jnp.concatenate([kg[:, 128:192], jnp.zeros((64, 64), BF)], axis=1)


def block(fields, cotangent, hal, params):
    index = [jnp.asarray(t) for t in static_tables()]
    tables = [jnp.asarray(t) for t in dft_tables()]
    vm = pl.BlockSpec(memory_space=pltpu.VMEM)
    args = [fields, cotangent, hal, *index, *tables, *params]
    return pl.pallas_call(
        block_kernel,
        out_shape=(
            jax.ShapeDtypeStruct((SIDE, SIDE, CH), BF),
            jax.ShapeDtypeStruct((SIDE, SIDE, CH), BF),
            jax.ShapeDtypeStruct(PACKED, BF),
            jax.ShapeDtypeStruct((WROWS, 128), BF),
        ),
        in_specs=[vm] * len(args),
        out_specs=(vm,) * 4,
        scratch_shapes=[
            pltpu.VMEM((EXT, KROW, CH), BF),
            pltpu.VMEM((EXT, 3 * NFREQ, CH), F32),
            pltpu.VMEM((EXT, 2 * NFREQ, CH), BF),
            pltpu.VMEM((SIDE + 12, 4 * NFREQ, CH), F32),
            pltpu.VMEM((8, CH), F32),
            pltpu.VMEM((7, 6 * NFREQ, CH), F32),
            pltpu.VMEM((7, 3 * NFREQ, CH), F32),
            pltpu.VMEM((CH, HID), F32),
            pltpu.VMEM((CH, HID), F32),
            pltpu.VMEM((SIDE, 16, CH), BF),
            pltpu.VMEM((W, KROW, CH), BF),
            pltpu.VMEM((W, KROW, CH), BF),
        ],
        compiler_params=pltpu.CompilerParams(vmem_limit_bytes=60 * 2**20),
        name="block",
    )(*args)


def last_kernel(scale, direct, bands, wsum, by_row, out, kgrad, egrad, rgrad):
    north = dot(spread(by_row, "north", W * SIDE), bands[0]).reshape(W, SIDE, CH)
    south = dot(spread(by_row, "south", W * SIDE), bands[2]).reshape(W, SIDE, CH)
    east = dot(spread(by_row, "east", 1024), bands[1]).reshape(SIDE, 16, CH)
    west = dot(spread(by_row, "west", 1024), bands[3]).reshape(SIDE, 16, CH)
    mid = slice(W, SIDE - W)
    out[mid, 16:48] = direct[mid, 16:48]
    out[mid, 0:16] = (direct[mid, 0:16].astype(F32) + west[mid]).astype(BF)
    out[mid, 48:64] = (direct[mid, 48:64].astype(F32) + east[mid]).astype(BF)
    zero = jnp.zeros((W, 32, CH), F32)
    for rows, add in ((slice(0, W), north), (slice(SIDE - W, SIDE), south)):
        more = jnp.concatenate([west[rows], zero, east[rows]], axis=1)
        out[rows] = (direct[rows].astype(F32) + add + more).astype(BF)
    for g in range(3):
        lanes = slice(128 * g, 128 * g + 128)
        egrad[:, lanes] = wsum[192 * g : 192 * g + 192].astype(F32) * scale
        rgrad[:, lanes] = wsum[576 + 192 * g : 768 + 192 * g].astype(F32) * scale
    low = wsum[1152:1216].astype(F32) * scale
    high = wsum[1216:1280].astype(F32) * scale
    for u in range(7):
        kgrad[u, :, 0:128] = low[8 * u : 8 * u + 7]
        kgrad[u, :, 128:192] = high[8 * u : 8 * u + 7, 0:64]


def last(direct, bands, wsum, scale):
    by_row, _ = static_tables()
    vm = pl.BlockSpec(memory_space=pltpu.VMEM)
    return pl.pallas_call(
        functools.partial(last_kernel, scale),
        out_shape=(
            jax.ShapeDtypeStruct((SIDE, SIDE, CH), BF),
            jax.ShapeDtypeStruct((7, 7, CH), F32),
            jax.ShapeDtypeStruct((CH, HID), F32),
            jax.ShapeDtypeStruct((CH, HID), F32),
        ),
        in_specs=[vm] * 4,
        out_specs=(vm,) * 4,
        compiler_params=pltpu.CompilerParams(vmem_limit_bytes=24 * 2**20),
        name="last",
    )(direct, bands, wsum, jnp.asarray(by_row))


def routing(neighbors, rotations):
    me = lax.axis_index("tile")
    offsets = jnp.array(OFFSETS, jnp.int32)[None, :]
    side = (rotations + offsets) % 4
    base = jnp.where(neighbors >= 0, side * 256 + neighbors * CELLS, -(1 << 20)).T
    right = jnp.where(me >= 7, 11, -(1 << 20))
    left = jnp.where(me <= 8, 0, -(1 << 20))
    corner_row = jnp.stack([right, left, right, left])[:, None]
    cell = jnp.arange(CELLS, dtype=jnp.int32)[None, None, :]
    edge = base[0:4][:, :, None] + cell
    corner = (base[4:8] + corner_row)[:, :, None]
    return jnp.where(cell < 12, edge, jnp.where(cell == 12, corner, -1)).astype(jnp.int32)


def on_device(
    fields,
    cotangent,
    kernel,
    conv_bias,
    norm_gain,
    norm_bias,
    w_expand,
    bias_expand,
    w_reduce,
    bias_reduce,
    layer_scale,
    neighbors,
    rotations,
):
    ndp = lax.axis_size("dp")
    field = fields.reshape(SIDE, SIDE, CH)
    cot = cotangent.reshape(SIDE, SIDE, CH)
    target = routing(neighbors, rotations)
    hal = halo(field, target.reshape(1024, 1))
    params = [
        kernel,
        conv_bias,
        norm_gain,
        norm_bias,
        w_expand,
        bias_expand,
        w_reduce.T,
        bias_reduce,
        layer_scale,
    ]
    mixed, direct, slots, wgrad = block(field, cot, hal, params)
    bands, wsum = send_back(
        slots, target.reshape(1, 1024), wgrad.reshape(ndp, WROWS // ndp, 128), ndp
    )
    scale = 1.0 / math.sqrt(ndp * TILES * SIDE * SIDE)
    input_grad, kgrad, egrad, rgrad = last(direct, bands, wsum, scale)
    return (
        mixed.reshape(fields.shape),
        input_grad.reshape(fields.shape),
        kgrad,
        egrad,
        rgrad.T,
    )


def solution(mesh):
    split = P("dp", "tile", None, None, None)
    return jax.shard_map(
        on_device,
        mesh=mesh,
        in_specs=(split, split) + (P(),) * 11,
        out_specs=(split, split, P(), P(), P()),
        check_vma=False,
    )
```

time: 133 us -> 106 us (0.80)
  Pallas kernels: 116 us -> 96.5 us
  local copies, waits for them, and re-layouts: 14.1 us -> 7.21 us
    pallas_call x1, Pallas kernels: 52 us -> 40.4 us  [block(): pl.pallas_call(block_kernel, out_shape=(jax.ShapeDtypeStruct((SIDE, SIDE,...]
    pallas_call x1, Pallas kernels: 37 us -> 30.8 us  [send_back(): pl.pallas_call(return_kernel, out_shape=(jax.ShapeDtypeStruct((4, 256, CH...]
    unnamed x28 -> x14, local copies, waits for them, and re-layouts: 12.5 us -> 6.83 us
    pallas_call x1, Pallas kernels: 25.4 us -> 23.4 us  [halo(): pl.pallas_call(halo_kernel, out_shape=jax.ShapeDtypeStruct((4, 256, CH),...]
where the time goes in v2:
time: 106 us; the launch traced here: 105 us
  Pallas kernels  96.5 us (91%)
  local copies, waits for them, and re-layouts  7.21 us (7%)
    pallas_call x1, Pallas kernels, block(): pl.pallas_call(block_kernel, out_shape=(jax.ShapeDtypeStruct((SIDE, SIDE,...  40.4 us
    pallas_call x1, Pallas kernels, send_back(): pl.pallas_call(return_kernel, out_shape=(jax.ShapeDtypeStruct((4, 256, CH...  30.8 us
    pallas_call x1, Pallas kernels, halo(): pl.pallas_call(halo_kernel, out_shape=jax.ShapeDtypeStruct((4, 256, CH),...  23.4 us
    unnamed x14, local copies, waits for them, and re-layouts  6.83 us

profile of v2, /device:TPU:1, one launch (start us, length us, event | category | flops | bytes accessed | tf_op | source)
XLA Modules:
  0.0 105.5 jit_solution(12977673684049586810)
XLA Ops:
  0.6 0.1 pad_add_fusion
  0.7 0.8 fusion.4
  1.5 0.1 fusion.5
  1.6 0.1 select_select_fusion
  1.7 0.1 select_n.69.target
  1.8 0.3 select_n.70.target
  2.1 0.0 copy-start
  2.1 1.6 %copy-done = bf16[1,1,64,64,192]{4,3,2,1,0:T(8,128)(2,1)S(1)} copy-done((bf16[1,1,64,64,192]{4,3,2,1,0:T(8,128)(2,1)S(1)}, bf16[1,1,64,64,192]{4,3,2,1,0:T(8,128)(2,1)}, u32[]{:S(2)}) %copy-start) | copy-done | bytes 1572888
  3.7 0.0 copy-start.3
  3.7 0.9 copy-done.3
  4.6 23.4 %halo.1.hal = bf16[4,256,192]{2,1,0:T(8,128)(2,1)S(1)} custom-call(bf16[64,64,192]{2,1,0:T(8,128)(2,1)S(1)} %bitcast.12, s32[256,128]{1,0:T(8,128)S(1)} %copy-done.3, s32[1024,1]{1,0:T(8,128)S(1)} %select_n.70.target), custom_call_target="tpu_custom_call" | custom-call | tf_op jit(solution)/shard_map/halo/pallas_call | solution.py:276
  27.9 0.0 copy-start.1
  27.9 0.8 copy-done.1
  28.7 0.0 copy-start.6
  28.7 40.4 %block.1 = (bf16[64,64,192]{2,1,0:T(8,128)(2,1)}, bf16[64,64,192]{2,1,0:T(8,128)(2,1)}, bf16[6,16,16,128]{3,2,1,0:T(8,128)(2,1)}, bf16[1280,128]{1,0:T(8,128)(2,1)}) custom-call(bf16[64,64,192]{2,1,0:T(8,128)(2,1)} %bitcast.11, bf16[64,64,192]{2,1,0:T(8,128)(2,1)} %bitcast.14, bf16[4,256,192]{2,1,0:T(8,128)(2,1)} %copy-done.1, ...), custom_call_target="tpu_custom_call" | custom-call | tf_op jit(solution)/shard_map/block/pallas_call | solution.py:634
  69.1 0.0 copy-start.4
  69.1 1.0 copy-done.4
  70.1 0.0 copy-start.5
  70.1 1.0 copy-done.5
  71.1 30.8 %send_back.1 = (bf16[4,256,192]{2,1,0:T(8,128)(2,1)S(1)}, bf16[1280,128]{1,0:T(8,128)(2,1)S(1)}) custom-call(bf16[6,16,16,128]{3,2,1,0:T(8,128)(2,1)S(1)} %copy-done.4, s32[1,1024]{1,0:T(1,128)S(1)} %select_n.69.target, bf16[8,160,128]{2,1,0:T(8,128)(2,1)S(1)} %bitcast.13), custom_call_target="tpu_custom_call" | custom-call | tf_op jit(solution)/shard_map/send_back/pallas_call | solution.py:380
  101.9 0.0 copy-done.6
  101.9 0.0 copy-start.2
  101.9 1.6 %copy-done.2 = bf16[64,64,192]{2,1,0:T(8,128)(2,1)S(1)} copy-done((bf16[64,64,192]{2,1,0:T(8,128)(2,1)S(1)}, bf16[64,64,192]{2,1,0:T(8,128)(2,1)}, u32[]{:S(2)}) %copy-start.2) | copy-done | bytes 1572888
  103.5 2.0 %last.1 = (bf16[64,64,192]{2,1,0:T(8,128)(2,1)}, f32[7,7,192]{2,1,0:T(8,128)}, f32[192,384]{1,0:T(8,128)}, f32[192,384]{1,0:T(8,128)}) custom-call(bf16[64,64,192]{2,1,0:T(8,128)(2,1)S(1)} %copy-done.2, bf16[4,256,192]{2,1,0:T(8,128)(2,1)S(1)} %get-tuple-element.19.bands, bf16[1280,128]{1,0:T(8,128)(2,1)S(1)} %get-tuple-element.20.wsum, s32[16,256]{1,0:T(8,128)S(1)} %copy-done.6), custom_call_target="tpu_custom_call" | custom-call | tf_op jit(solution)/shard_map/last/pallas_call | solution.py:690
  (1 shorter events, 0.0 us)
Async XLA Ops:
  2.1 1.6 %copy-start = (bf16[1,1,64,64,192]{4,3,2,1,0:T(8,128)(2,1)S(1)}, bf16[1,1,64,64,192]{4,3,2,1,0:T(8,128)(2,1)}, u32[]{:S(2)}) copy-start(bf16[1,1,64,64,192]{4,3,2,1,0:T(8,128)(2,1)} %param.22) | copy-start | bytes 4718596
  3.7 0.9 copy-start.3
  27.9 0.8 copy-start.1
  28.7 73.1 %copy-start.6 = (s32[16,256]{1,0:T(8,128)S(1)}, s32[16,256]{1,0:T(8,128)}, u32[]{:S(2)}) copy-start(s32[16,256]{1,0:T(8,128)} %constant.57.clone.by_row) | copy-start | bytes 49156
  69.1 1.0 copy-start.4
  70.1 1.0 copy-start.5
  101.9 1.6 %copy-start.2 = (bf16[64,64,192]{2,1,0:T(8,128)(2,1)S(1)}, bf16[64,64,192]{2,1,0:T(8,128)(2,1)}, u32[]{:S(2)}) copy-start(bf16[64,64,192]{2,1,0:T(8,128)(2,1)} %get-tuple-element.16.direct) | copy-start | bytes 4718596

commit v3 on v2

--- a/solution.py
+++ b/solution.py
@@ -242,171 +242,6 @@
     return jnp.concatenate([low, high], axis=-1)
 
 
-def halo_kernel(field, by_col, target, out, own, got, routed, back, s1, r1, s2, r2):
-    me = lax.axis_index("tile")
-    barrier, total = greet((("tile", TILES),))
-    bands = jnp.concatenate(
-        [
-            dot(gather(by_col, "north", W * SIDE), field[0:W].reshape(W * SIDE, CH)),
-            dot(gather(by_col, "east", 1024), field[:, 48:64].reshape(1024, CH)),
-            dot(gather(by_col, "south", W * SIDE), field[SIDE - W :].reshape(W * SIDE, CH)),
-            dot(gather(by_col, "west", 1024), field[:, 0:16].reshape(1024, CH)),
-        ],
-        axis=0,
-    )
-    pack(own, bands.astype(BF).reshape(4, TILES, CELLS, CH))
-    pl.semaphore_wait(barrier, total)
-    copies = exchange("tile", TILES, lambda to: own.at[:, to], lambda m: got.at[:, m], s1, r1)
-    got[:, me] = own[:, me]
-    columns = lax.broadcasted_iota(jnp.int32, (1024, 1024), 1)
-    route = (columns == target[...]).astype(F32).astype(BF)
-    finish(copies)
-    pack(routed, dot(route, unpack(got)).astype(BF).reshape(4, TILES, CELLS, CH))
-    copies = exchange("tile", TILES, lambda to: routed.at[:, to], lambda m: back.at[:, m], s2, r2)
-    back[:, me] = routed[:, me]
-    finish(copies)
-    out[...] = unpack(back).reshape(4, 256, CH)
-
-
-def halo(fields, target_col):
-    _, by_col = static_tables()
-    vm = pl.BlockSpec(memory_space=pltpu.VMEM)
-    block = pltpu.VMEM(PACKED, BF)
-    sem = pltpu.SemaphoreType.DMA((TILES,))
-    return pl.pallas_call(
-        halo_kernel,
-        out_shape=jax.ShapeDtypeStruct((4, 256, CH), BF),
-        in_specs=[vm] * 3,
-        out_specs=vm,
-        scratch_shapes=[block, block, block, block, sem, sem, sem, sem],
-        compiler_params=pltpu.CompilerParams(
-            collective_id=0, has_side_effects=True, vmem_limit_bytes=24 * 2**20
-        ),
-        name="halo",
-    )(fields, jnp.asarray(by_col), target_col)
-
-
-def return_kernel(
-    slots, target, wsrc, out, wout, got, routed, back, wa, pa, wb, pc, wc, wd, *sems
-):
-    s1, r1, s2, r2, sa, ra, sb, rb, sc, rc, sd, rd = sems
-    me = lax.axis_index("tile")
-    md = lax.axis_index("dp")
-    ndp = wa.shape[0]
-    owners = pa.shape[0]
-    barrier, total = greet((("tile", TILES), ("dp", ndp)))
-    pl.semaphore_wait(barrier, total)
-    ca = exchange("dp", ndp, lambda to: wsrc.at[to], lambda m: wa.at[m], sa, ra)
-    c1 = exchange("tile", TILES, lambda to: slots.at[:, to], lambda m: got.at[:, m], s1, r1)
-    got[:, me] = slots[:, me]
-    wa[md] = wsrc[md]
-    rows = lax.broadcasted_iota(jnp.int32, (1024, 1024), 0)
-    route = (rows == target[...]).astype(F32).astype(BF)
-
-    finish(ca)
-    part = wa[0].astype(F32)
-    for j in range(1, ndp):
-        part = part + wa[j].astype(F32)
-    pa[...] = part.reshape(owners, WBLOCK, 128)
-
-    def share(off, src, dst, send, recv):
-        to = peer(me, off, TILES)
-        return pltpu.make_async_remote_copy(
-            src_ref=src,
-            dst_ref=dst,
-            send_sem=send.at[off],
-            recv_sem=recv.at[off],
-            device_id={"tile": to},
-            device_id_type=MESH,
-        )
-
-    def to_owner(off):
-        to = peer(me, off, TILES)
-        return to, share(off, pa.at[lax.rem(to, owners)], wb.at[me], sb, rb)
-
-    for off in range(1, TILES):
-        to, copy = to_owner(off)
-        pl.when(to < owners)(copy.start)
-
-    @pl.when(me < owners)
-    def _():
-        wb[me] = pa[lax.rem(me, owners)]
-
-    finish(c1)
-    pack(routed, dot(route, unpack(got)).astype(BF).reshape(4, TILES, CELLS, CH))
-    c2 = exchange("tile", TILES, lambda to: routed.at[:, to], lambda m: back.at[:, m], s2, r2)
-    back[:, me] = routed[:, me]
-
-    for off in range(1, TILES):
-        to, copy = to_owner(off)
-        pl.when(to < owners)(copy.wait_send)
-        pl.when(me < owners)(copy.wait_recv)
-
-    mine = lax.rem(me, owners)
-
-    @pl.when(me < owners)
-    def _():
-        total = wb[0]
-        for j in range(1, TILES):
-            total = total + wb[j]
-        pc[...] = total.astype(BF)
-        wc[mine] = total.astype(BF)
-        for off in range(1, TILES):
-            share(off, pc, wc.at[mine], sc, rc).start()
-
-    for off in range(1, TILES):
-        copy = share(off, pc, wc.at[mine], sc, rc)
-        pl.when(me < owners)(copy.wait_send)
-        pl.when(peer(me, TILES - off, TILES) < owners)(copy.wait_recv)
-
-    block = wc[...].reshape(owners * WBLOCK, 128)
-    pd = wa.at[0]
-    pd[...] = block
-    cd = exchange("dp", ndp, lambda to: pd, lambda m: wd.at[m], sd, rd)
-    wd[md] = block
-    finish(c2)
-    out[...] = unpack(back).reshape(4, 256, CH)
-    finish(cd)
-    wout[...] = wd[...].reshape(WROWS, 128)
-
-
-def send_back(slots, target_row, wsrc, ndp):
-    vm = pl.BlockSpec(memory_space=pltpu.VMEM)
-    block = pltpu.VMEM(PACKED, BF)
-    sem = pltpu.SemaphoreType.DMA((TILES,))
-    sem_dp = pltpu.SemaphoreType.DMA((ndp,))
-    dp_rows = WROWS // ndp
-    owners = dp_rows // WBLOCK
-    return pl.pallas_call(
-        return_kernel,
-        out_shape=(
-            jax.ShapeDtypeStruct((4, 256, CH), BF),
-            jax.ShapeDtypeStruct((WROWS, 128), BF),
-        ),
-        in_specs=[vm] * 3,
-        out_specs=(vm, vm),
-        scratch_shapes=[
-            block,
-            block,
-            block,
-            pltpu.VMEM((ndp, dp_rows, 128), BF),
-            pltpu.VMEM((owners, WBLOCK, 128), F32),
-            pltpu.VMEM((TILES, WBLOCK, 128), F32),
-            pltpu.VMEM((WBLOCK, 128), BF),
-            pltpu.VMEM((owners, WBLOCK, 128), BF),
-            pltpu.VMEM((ndp, dp_rows, 128), BF),
-        ]
-        + [sem] * 4
-        + [sem_dp] * 2
-        + [sem] * 4
-        + [sem_dp] * 2,
-        compiler_params=pltpu.CompilerParams(
-            collective_id=1, has_side_effects=True, vmem_limit_bytes=24 * 2**20
-        ),
-        name="send_back",
-    )(slots, target_row, wsrc)
-
-
 LANES = ((0, 128), (128, 64))
 
 
@@ -421,12 +256,13 @@
     return jnp.concatenate([a - b, c - a - b], axis=0).astype(BF)
 
 
-def block_kernel(
+def main_kernel(
     fields,
-    cot,
-    hal,
+    cot_hbm,
     by_row,
     by_col,
+    target_col,
+    target_row,
     fwd_x,
     inv_y,
     fwd_g,
@@ -444,7 +280,7 @@
     lscale,
     mixed,
     direct,
-    slots,
+    bands,
     wout,
     xpad,
     x3,
@@ -458,7 +294,49 @@
     psides,
     ptop,
     pbot,
+    cot,
+    mix_out,
+    hal,
+    own,
+    got,
+    routed,
+    back,
+    own2,
+    got2,
+    routed2,
+    back2,
+    wsrc,
+    wa,
+    pa,
+    wb,
+    pc,
+    wc,
+    wd,
+    io_sem,
+    *sems,
 ):
+    s1, r1, s2, r2, s3, r3, s4, r4, sb, rb, sc, rc, sa, ra, sd, rd = sems
+    me = lax.axis_index("tile")
+    md = lax.axis_index("dp")
+    ndp = wa.shape[0]
+    dp_rows = wa.shape[1]
+    owners = pa.shape[0]
+    barrier, total = greet((("tile", TILES), ("dp", ndp)))
+    load_cot = pltpu.make_async_copy(cot_hbm, cot, io_sem.at[0])
+    load_cot.start()
+    bands_own = jnp.concatenate(
+        [
+            dot(gather(by_col, "north", W * SIDE), fields[0:W].reshape(W * SIDE, CH)),
+            dot(gather(by_col, "east", 1024), fields[:, 48:64].reshape(1024, CH)),
+            dot(gather(by_col, "south", W * SIDE), fields[SIDE - W :].reshape(W * SIDE, CH)),
+            dot(gather(by_col, "west", 1024), fields[:, 0:16].reshape(1024, CH)),
+        ],
+        axis=0,
+    )
+    pack(own, bands_own.astype(BF).reshape(4, TILES, CELLS, CH))
+    pl.semaphore_wait(barrier, total)
+    copies = exchange("tile", TILES, lambda to: own.at[:, to], lambda m: got.at[:, m], s1, r1)
+    got[:, me] = own[:, me]
     conv_bias, gain, nbias, b_exp, b_red, lscale = (
         ref[...].reshape(1, -1) for ref in (conv_bias, gain, nbias, b_exp, b_red, lscale)
     )
@@ -466,7 +344,17 @@
         kpad[0:7] = kernel[u]
         kpad[7:8] = jnp.zeros((1, CH), F32)
         kf[u] = dot_exact(fwd_k[...], kpad[...])
+    g4[0:6] = jnp.zeros((6, 4 * NFREQ, CH), F32)
+    g4[6 + SIDE :] = jnp.zeros((6, 4 * NFREQ, CH), F32)
     xpad[W : W + SIDE, 0:SIDE] = fields[...]
+    columns = lax.broadcasted_iota(jnp.int32, (1024, 1024), 1)
+    route = (columns == target_col[...]).astype(F32).astype(BF)
+    finish(copies)
+    pack(routed, dot(route, unpack(got)).astype(BF).reshape(4, TILES, CELLS, CH))
+    copies = exchange("tile", TILES, lambda to: routed.at[:, to], lambda m: back.at[:, m], s2, r2)
+    back[:, me] = routed[:, me]
+    finish(copies)
+    hal[...] = unpack(back).reshape(4, 256, CH)
 
     def put(n, *parts):
         return sum(dot(spread(by_row, name, n), hal[k]) for name, k in parts).astype(BF)
@@ -499,10 +387,9 @@
 
             lax.fori_loop(0, SIDE // 4, conv, 0, unroll=2)
 
+    load_cot.wait()
     egrad[...] = jnp.zeros_like(egrad)
     rgrad[...] = jnp.zeros_like(rgrad)
-    g4[0:6] = jnp.zeros((6, 4 * NFREQ, CH), F32)
-    g4[6 + SIDE :] = jnp.zeros((6, 4 * NFREQ, CH), F32)
     step = 16
     n = step * SIDE
 
@@ -531,7 +418,7 @@
         cot_c = cot[pl.ds(i0, step)].reshape(n, CH).astype(F32)
         branch = dot_nt(act, w_red[...]) + b_red
         mix = fields[pl.ds(i0, step)].reshape(n, CH).astype(F32) + lscale * branch
-        mixed[pl.ds(i0, step)] = mix.astype(BF).reshape(step, SIDE, CH)
+        mix_out[pl.ds(i0, step)] = mix.astype(BF).reshape(step, SIDE, CH)
         bgrad = (lscale * cot_c).astype(BF)
         pre_grad = (dot(bgrad, w_red[...]) * slope).astype(BF)
         rgrad[...] += dot_tn(bgrad, act)
@@ -546,6 +433,9 @@
 
     lax.fori_loop(0, SIDE // step, chunk, 0)
 
+    store_mixed = pltpu.make_async_copy(mix_out, mixed, io_sem.at[1])
+    store_mixed.start()
+
     for l0, lw in LANES:
         for fb in range(5):
             rows = [slice(40 * t + 8 * fb, 40 * t + 8 * fb + 8) for t in range(4)]
@@ -569,6 +459,27 @@
                 for u in range(7):
                     m3[u, rows[t], lanes] = accs[7 * t + u]
 
+
+    for g in range(3):
+        lanes = slice(128 * g, 128 * g + 128)
+        wsrc[192 * g : 192 * g + 192] = egrad[:, lanes].astype(BF)
+        wsrc[576 + 192 * g : 768 + 192 * g] = rgrad[:, lanes].astype(BF)
+    kg = jnp.concatenate([dot_exact(inv_k[...], m3[u]) for u in range(7)], axis=0)
+    kg = jnp.concatenate([kg, jnp.zeros((8, CH), F32)], axis=0).astype(BF)
+    wsrc[1152:1216] = kg[:, 0:128]
+    wsrc[1216:1280] = jnp.concatenate([kg[:, 128:192], jnp.zeros((64, 64), BF)], axis=1)
+
+    def dp_block(to):
+        return wsrc.at[pl.ds(pl.multiple_of(to * dp_rows, 16), dp_rows)]
+
+    ca = exchange("dp", ndp, dp_block, lambda m: wa.at[m], sa, ra)
+    wa[md] = wsrc[pl.ds(pl.multiple_of(md * dp_rows, 16), dp_rows)]
+
+    for l0, lw in LANES:
+        for fb in range(5):
+            rows = [slice(40 * t + 8 * fb, 40 * t + 8 * fb + 8) for t in range(3)]
+            lanes = slice(l0, l0 + lw)
+
             kk = [
                 [kf[u, 120 + 40 * t + 8 * fb : 128 + 40 * t + 8 * fb, lanes] for t in range(3)]
                 for u in range(7)
@@ -587,6 +498,35 @@
 
             lax.fori_loop(0, EXT // 5, pconv, 0, unroll=2)
 
+
+    finish(ca)
+    part = wa[0].astype(F32)
+    for j in range(1, ndp):
+        part = part + wa[j].astype(F32)
+    pa[...] = part.reshape(owners, WBLOCK, 128)
+
+    def share(off, src, dst, send, recv):
+        return pltpu.make_async_remote_copy(
+            src_ref=src,
+            dst_ref=dst,
+            send_sem=send.at[off],
+            recv_sem=recv.at[off],
+            device_id={"tile": peer(me, off, TILES)},
+            device_id_type=MESH,
+        )
+
+    def to_owner(off):
+        to = peer(me, off, TILES)
+        return to, share(off, pa.at[lax.rem(to, owners)], wb.at[me], sb, rb)
+
+    for off in range(1, TILES):
+        to, copy = to_owner(off)
+        pl.when(to < owners)(copy.start)
+
+    @pl.when(me < owners)
+    def _():
+        wb[me] = pa[lax.rem(me, owners)]
+
     for p in range(W):
         ptop[p] = dot(inv_p[...], y2[p]).astype(BF)
         pbot[p] = dot(inv_p[...], y2[W + SIDE + p]).astype(BF)
@@ -614,33 +554,74 @@
         take(("bot2", bot)),
         take(("side3", sides), ("top3", top)),
     ]
-    pack(slots, jnp.concatenate(taken, axis=0))
-
-    for g in range(3):
-        lanes = slice(128 * g, 128 * g + 128)
-        wout[192 * g : 192 * g + 192] = egrad[:, lanes].astype(BF)
-        wout[576 + 192 * g : 768 + 192 * g] = rgrad[:, lanes].astype(BF)
-    kg = jnp.concatenate([dot_exact(inv_k[...], m3[u]) for u in range(7)], axis=0)
-    kg = jnp.concatenate([kg, jnp.zeros((8, CH), F32)], axis=0).astype(BF)
-    wout[1152:1216] = kg[:, 0:128]
-    wout[1216:1280] = jnp.concatenate([kg[:, 128:192], jnp.zeros((64, 64), BF)], axis=1)
-
-
-def block(fields, cotangent, hal, params):
+    pack(own2, jnp.concatenate(taken, axis=0))
+
+
+    c3 = exchange("tile", TILES, lambda to: own2.at[:, to], lambda m: got2.at[:, m], s3, r3)
+    got2[:, me] = own2[:, me]
+    for off in range(1, TILES):
+        to, copy = to_owner(off)
+        pl.when(to < owners)(copy.wait_send)
+        pl.when(me < owners)(copy.wait_recv)
+
+    mine = lax.rem(me, owners)
+
+    @pl.when(me < owners)
+    def _():
+        whole = wb[0]
+        for j in range(1, TILES):
+            whole = whole + wb[j]
+        pc[...] = whole.astype(BF)
+        wc[mine] = whole.astype(BF)
+        for off in range(1, TILES):
+            share(off, pc, wc.at[mine], sc, rc).start()
+
+    rows = lax.broadcasted_iota(jnp.int32, (1024, 1024), 0)
+    route_back = (rows == target_row[...]).astype(F32).astype(BF)
+    for off in range(1, TILES):
+        copy = share(off, pc, wc.at[mine], sc, rc)
+        pl.when(me < owners)(copy.wait_send)
+        pl.when(peer(me, TILES - off, TILES) < owners)(copy.wait_recv)
+
+    block = wc[...].reshape(owners * WBLOCK, 128)
+    pd = wa.at[0]
+    pd[...] = block
+    cd = exchange("dp", ndp, lambda to: pd, lambda m: wd.at[m], sd, rd)
+    wd[md] = block
+    finish(c3)
+    pack(routed2, dot(route_back, unpack(got2)).astype(BF).reshape(4, TILES, CELLS, CH))
+    c4 = exchange("tile", TILES, lambda to: routed2.at[:, to], lambda m: back2.at[:, m], s4, r4)
+    back2[:, me] = routed2[:, me]
+    finish(cd)
+    wout[...] = wd[...].reshape(WROWS, 128)
+    finish(c4)
+    bands[...] = unpack(back2).reshape(4, 256, CH)
+    store_mixed.wait()
+
+
+def main(fields, cotangent, target, params, ndp):
     index = [jnp.asarray(t) for t in static_tables()]
     tables = [jnp.asarray(t) for t in dft_tables()]
     vm = pl.BlockSpec(memory_space=pltpu.VMEM)
-    args = [fields, cotangent, hal, *index, *tables, *params]
+    hbm = pl.BlockSpec(memory_space=pl.ANY)
+    halo_buf = pltpu.VMEM(PACKED, BF)
+    sem = pltpu.SemaphoreType.DMA((TILES,))
+    sem_dp = pltpu.SemaphoreType.DMA((ndp,))
+    dp_rows = WROWS // ndp
+    owners = dp_rows // WBLOCK
+    targets = [target.reshape(1024, 1), target.reshape(1, 1024)]
+    args = [fields, cotangent, *index, *targets, *tables, *params]
+    field = jax.ShapeDtypeStruct((SIDE, SIDE, CH), BF)
     return pl.pallas_call(
-        block_kernel,
+        main_kernel,
         out_shape=(
-            jax.ShapeDtypeStruct((SIDE, SIDE, CH), BF),
-            jax.ShapeDtypeStruct((SIDE, SIDE, CH), BF),
-            jax.ShapeDtypeStruct(PACKED, BF),
+            field,
+            field,
+            jax.ShapeDtypeStruct((4, 256, CH), BF),
             jax.ShapeDtypeStruct((WROWS, 128), BF),
         ),
-        in_specs=[vm] * len(args),
-        out_specs=(vm,) * 4,
+        in_specs=[vm, hbm] + [vm] * (len(args) - 2),
+        out_specs=(hbm, vm, vm, vm),
         scratch_shapes=[
             pltpu.VMEM((EXT, KROW, CH), BF),
             pltpu.VMEM((EXT, 3 * NFREQ, CH), F32),
@@ -654,9 +635,27 @@
             pltpu.VMEM((SIDE, 16, CH), BF),
             pltpu.VMEM((W, KROW, CH), BF),
             pltpu.VMEM((W, KROW, CH), BF),
-        ],
-        compiler_params=pltpu.CompilerParams(vmem_limit_bytes=60 * 2**20),
-        name="block",
+            pltpu.VMEM((SIDE, SIDE, CH), BF),
+            pltpu.VMEM((SIDE, SIDE, CH), BF),
+            pltpu.VMEM((4, 256, CH), BF),
+        ]
+        + [halo_buf] * 8
+        + [
+            pltpu.VMEM((WROWS, 128), BF),
+            pltpu.VMEM((ndp, dp_rows, 128), BF),
+            pltpu.VMEM((owners, WBLOCK, 128), F32),
+            pltpu.VMEM((TILES, WBLOCK, 128), F32),
+            pltpu.VMEM((WBLOCK, 128), BF),
+            pltpu.VMEM((owners, WBLOCK, 128), BF),
+            pltpu.VMEM((ndp, dp_rows, 128), BF),
+            pltpu.SemaphoreType.DMA((2,)),
+        ]
+        + [sem] * 12
+        + [sem_dp] * 4,
+        compiler_params=pltpu.CompilerParams(
+            collective_id=0, has_side_effects=True, vmem_limit_bytes=62 * 2**20
+        ),
+        name="main",
     )(*args)
 
 
@@ -735,7 +734,6 @@
     field = fields.reshape(SIDE, SIDE, CH)
     cot = cotangent.reshape(SIDE, SIDE, CH)
     target = routing(neighbors, rotations)
-    hal = halo(field, target.reshape(1024, 1))
     params = [
         kernel,
         conv_bias,
@@ -747,10 +745,7 @@
         bias_reduce,
         layer_scale,
     ]
-    mixed, direct, slots, wgrad = block(field, cot, hal, params)
-    bands, wsum = send_back(
-        slots, target.reshape(1, 1024), wgrad.reshape(ndp, WROWS // ndp, 128), ndp
-    )
+    mixed, direct, bands, wsum = main(field, cot, target, params, ndp)
     scale = 1.0 / math.sqrt(ndp * TILES * SIDE * SIDE)
     input_grad, kgrad, egrad, rgrad = last(direct, bands, wsum, scale)
     return (

time: 106 us -> 97.5 us (0.920)
  Pallas kernels: 96.5 us -> 88.8 us
    pallas_call x3 -> x1, Pallas kernels: 94.5 us -> 86.8 us  [main(): pl.pallas_call(main_kernel, out_shape=(field, field, jax.ShapeDtypeStruct...]
    unnamed x14 -> x11, local copies, waits for them, and re-layouts: 6.83 us -> 4.92 us
    select_n x2, local copies, waits for them, and re-layouts: 0.38 us -> 1.77 us  [routing(): jnp.where(cell < 12, edge, jnp.where(cell == 12, corner, -1))]
where the time goes in v3:
time: 97.5 us; the launch traced here: 97.2 us
  Pallas kernels  88.8 us (91%)
  local copies, waits for them, and re-layouts  6.7 us (7%)
  other arithmetic  1.02 us (1%)
    pallas_call x1, Pallas kernels, main(): pl.pallas_call(main_kernel, out_shape=(field, field, jax.ShapeDtypeStruct...  86.8 us
    unnamed x11, local copies, waits for them, and re-layouts  4.92 us
    pallas_call x1, Pallas kernels, last(): pl.pallas_call(functools.partial(last_kernel, scale), out_shape=(jax.Shap...  2.03 us

profile of v3, /device:TPU:1, one launch (start us, length us, event | category | flops | bytes accessed | tf_op | source)
XLA Modules:
  0.0 97.2 jit_solution(12612575504214249513)
XLA Ops:
  0.6 0.1 pad_add_fusion
  0.7 0.8 fusion.4
  1.5 0.1 fusion.5
  1.6 0.1 select_select_fusion
  1.7 0.7 select_n.69.target_row
  2.4 1.1 %select_n.70.target_col = s32[1024,1]{1,0:T(8,128)} reshape(s32[4,16,16]{2,1,0:T(8,128)S(1)} %select_select_fusion) | data formatting | bytes 8192 | tf_op jit(solution)/shard_map/jit(_where)/select_n | solution.py:715
  3.4 0.0 copy-start.3
  3.4 86.8 %main.1 = (bf16[64,64,192]{2,1,0:T(8,128)(2,1)}, bf16[64,64,192]{2,1,0:T(8,128)(2,1)}, bf16[4,256,192]{2,1,0:T(8,128)(2,1)}, bf16[1280,128]{1,0:T(8,128)(2,1)}) custom-call(bf16[64,64,192]{2,1,0:T(8,128)(2,1)} %bitcast.10, bf16[64,64,192]{2,1,0:T(8,128)(2,1)} %bitcast.11, s32[16,256]{1,0:T(8,128)} %constant.56.clone.by_row, ...), custom_call_target="tpu_custom_call" | custom-call | tf_op jit(solution)/shard_map/main/pallas_call | solution.py:615
  90.2 0.0 copy-done.3
  90.2 0.0 copy-start
  90.3 1.6 %copy-done = bf16[64,64,192]{2,1,0:T(8,128)(2,1)S(1)} copy-done((bf16[64,64,192]{2,1,0:T(8,128)(2,1)S(1)}, bf16[64,64,192]{2,1,0:T(8,128)(2,1)}, u32[]{:S(2)}) %copy-start) | copy-done | bytes 1572888
  91.8 0.0 copy-start.1
  91.8 1.0 %copy-done.1 = bf16[4,256,192]{2,1,0:T(8,128)(2,1)S(1)} copy-done((bf16[4,256,192]{2,1,0:T(8,128)(2,1)S(1)}, bf16[4,256,192]{2,1,0:T(8,128)(2,1)}, u32[]{:S(2)}) %copy-start.1) | copy-done | bytes 393240
  92.9 0.0 copy-start.2
  92.9 1.0 copy-done.2
  93.9 0.0 copy-start.4
  93.9 2.0 %last.1 = (bf16[64,64,192]{2,1,0:T(8,128)(2,1)}, f32[7,7,192]{2,1,0:T(8,128)}, f32[192,384]{1,0:T(8,128)}, f32[192,384]{1,0:T(8,128)}) custom-call(bf16[64,64,192]{2,1,0:T(8,128)(2,1)S(1)} %copy-done, bf16[4,256,192]{2,1,0:T(8,128)(2,1)S(1)} %copy-done.1, bf16[1280,128]{1,0:T(8,128)(2,1)S(1)} %copy-done.2, s32[16,256]{1,0:T(8,128)S(1)} %copy-done.3), custom_call_target="tpu_custom_call" | custom-call | tf_op jit(solution)/shard_map/last/pallas_call | solution.py:689
  95.9 0.0 copy-done.4
  95.9 1.3 %copy.29 = bf16[1,1,64,64,192]{4,3,2,1,0:T(8,128)(2,1)} copy(bf16[1,1,64,64,192]{4,3,2,1,0:T(8,128)(2,1)S(1)} %bitcast.12) | data formatting | bytes 3145728
  (1 shorter events, 0.0 us)
Async XLA Ops:
  3.4 86.8 %copy-start.3 = (s32[16,256]{1,0:T(8,128)S(1)}, s32[16,256]{1,0:T(8,128)}, u32[]{:S(2)}) copy-start(s32[16,256]{1,0:T(8,128)} %constant.56.clone.by_row) | copy-start | bytes 49156
  90.2 1.6 %copy-start = (bf16[64,64,192]{2,1,0:T(8,128)(2,1)S(1)}, bf16[64,64,192]{2,1,0:T(8,128)(2,1)}, u32[]{:S(2)}) copy-start(bf16[64,64,192]{2,1,0:T(8,128)(2,1)} %get-tuple-element.14.direct) | copy-start | bytes 4718596
  91.8 1.0 %copy-start.1 = (bf16[4,256,192]{2,1,0:T(8,128)(2,1)S(1)}, bf16[4,256,192]{2,1,0:T(8,128)(2,1)}, u32[]{:S(2)}) copy-start(bf16[4,256,192]{2,1,0:T(8,128)(2,1)} %get-tuple-element.15.bands) | copy-start | bytes 1179652
  92.9 1.0 %copy-start.2 = (bf16[1280,128]{1,0:T(8,128)(2,1)S(1)}, bf16[1280,128]{1,0:T(8,128)(2,1)}, u32[]{:S(2)}) copy-start(bf16[1280,128]{1,0:T(8,128)(2,1)} %get-tuple-element.16.wsum) | copy-start | bytes 983044
  93.9 2.0 %copy-start.4 = (bf16[64,64,192]{2,1,0:T(8,128)(2,1)S(1)}, bf16[64,64,192]{2,1,0:T(8,128)(2,1)}, u32[]{:S(2)}) copy-start(bf16[64,64,192]{2,1,0:T(8,128)(2,1)} %get-tuple-element.13) | copy-start | bytes 4718596

commit v4 on v3

--- a/solution.py
+++ b/solution.py
@@ -22,7 +22,8 @@
 BF = jnp.bfloat16
 F32 = jnp.float32
 MESH = pl.DeviceIdType.MESH
-WROWS = 1280
+WROWS = 1152
+KROWS = 128
 WBLOCK = 16
 INDEX = ("top0", "top3", "bot2", "bot1", "side3", "side1", "north", "east", "south", "west")
 
@@ -256,13 +257,37 @@
     return jnp.concatenate([a - b, c - a - b], axis=0).astype(BF)
 
 
+def route_targets(base, me, axis):
+    shape = (1024, 16) if axis == 0 else (16, 1024)
+    row = lax.broadcasted_iota(jnp.int32, shape, axis)
+    tile = lax.broadcasted_iota(jnp.int32, shape, 1 - axis)
+    pick = (((row >> 4) & 15) == tile).astype(F32).astype(BF)
+    found = dot_nt(pick, base) if axis == 0 else dot(base, pick)
+    slot = lax.broadcasted_iota(jnp.int32, found.shape, 1 - axis)
+    row = lax.broadcasted_iota(jnp.int32, found.shape, axis)
+    edge = jnp.sum(jnp.where(slot == row >> 8, found, 0.0), axis=1 - axis, keepdims=True)
+    corner = jnp.sum(jnp.where(slot == (row >> 8) + 4, found, 0.0), axis=1 - axis, keepdims=True)
+    row = lax.broadcasted_iota(jnp.int32, edge.shape, axis)
+    cell = row & 15
+    right = jnp.where(me >= 7, 11.0, -8192.0)
+    left = jnp.where(me <= 8, 0.0, -8192.0)
+    corner = corner + jnp.where((row >> 8) & 1 == 0, right, left)
+    return jnp.where(cell < 12, edge + cell.astype(F32), jnp.where(cell == 12, corner, -1.0))
+
+
+def route_matrix(base, me, axis):
+    place = lax.broadcasted_iota(jnp.int32, (1024, 1024), 1 - axis).astype(F32)
+    return (place == route_targets(base, me, axis)).astype(F32).astype(BF)
+
+
 def main_kernel(
     fields,
     cot_hbm,
     by_row,
     by_col,
-    target_col,
-    target_row,
+    neighbors,
+    rotations,
+    offsets,
     fwd_x,
     inv_y,
     fwd_g,
@@ -312,15 +337,30 @@
     pc,
     wc,
     wd,
+    ksrc,
+    kwa,
+    kpart,
+    kwb,
+    kwhole,
+    kwc,
+    dir_out,
     io_sem,
     *sems,
 ):
-    s1, r1, s2, r2, s3, r3, s4, r4, sb, rb, sc, rc, sa, ra, sd, rd = sems
+    s1, r1, s2, r2, s3, r3, s4, r4, sb, rb, sc, rc, skb, rkb = sems[:14]
+    sa, ra, sd, rd, ska, rka, skc, rkc = sems[14:]
     me = lax.axis_index("tile")
     md = lax.axis_index("dp")
     ndp = wa.shape[0]
     dp_rows = wa.shape[1]
+    krows = kpart.shape[0]
     owners = pa.shape[0]
+    base = jnp.where(
+        neighbors[...] >= 0,
+        ((rotations[...] + offsets[...]) & 3) * 256 + neighbors[...] * CELLS,
+        -4096,
+    )
+    base = base.astype(F32).astype(BF)
     barrier, total = greet((("tile", TILES), ("dp", ndp)))
     load_cot = pltpu.make_async_copy(cot_hbm, cot, io_sem.at[0])
     load_cot.start()
@@ -347,8 +387,7 @@
     g4[0:6] = jnp.zeros((6, 4 * NFREQ, CH), F32)
     g4[6 + SIDE :] = jnp.zeros((6, 4 * NFREQ, CH), F32)
     xpad[W : W + SIDE, 0:SIDE] = fields[...]
-    columns = lax.broadcasted_iota(jnp.int32, (1024, 1024), 1)
-    route = (columns == target_col[...]).astype(F32).astype(BF)
+    route = route_matrix(base, me, 0)
     finish(copies)
     pack(routed, dot(route, unpack(got)).astype(BF).reshape(4, TILES, CELLS, CH))
     copies = exchange("tile", TILES, lambda to: routed.at[:, to], lambda m: back.at[:, m], s2, r2)
@@ -390,20 +429,23 @@
     load_cot.wait()
     egrad[...] = jnp.zeros_like(egrad)
     rgrad[...] = jnp.zeros_like(rgrad)
-    step = 16
+    step = 4
+    parts = 8
     n = step * SIDE
 
-    def chunk(ic, _):
-        i0 = pl.multiple_of(ic * step, step)
-        conv_out = jnp.concatenate(
-            [dot(inv_y[...], y2[i0 + d]) for d in range(step)], axis=0
-        )
+    def part(i0):
+        conv_out = jnp.concatenate([dot(inv_y[...], y2[i0 + d]) for d in range(step)], axis=0)
+        yield
         conv_out = conv_out + conv_bias
         shifted = conv_out - jnp.mean(conv_out, axis=-1, keepdims=True)
         inv_std = lax.rsqrt(jnp.mean(shifted * shifted, axis=-1, keepdims=True) + 1e-06)
         centred = shifted * inv_std
         normed = (centred * gain + nbias).astype(BF)
+        yield
         pre = dot(normed, w_exp[...]) + b_exp
+        bgrad = (lscale * cot[pl.ds(i0, step)].reshape(n, CH).astype(F32)).astype(BF)
+        act_grad = dot(bgrad, w_red[...])
+        yield
         size = jnp.abs(pre)
         t = 1.0 / (1.0 + (0.3275911 * math.sqrt(0.5)) * size)
         dens = jnp.exp(-0.5 * pre * pre)
@@ -414,27 +456,150 @@
         tail = poly * dens
         phi = jnp.where(pre >= 0, 1.0 - tail, tail)
         act = (pre * phi).astype(BF)
-        slope = phi + pre * (dens * 0.3989422804014327)
-        cot_c = cot[pl.ds(i0, step)].reshape(n, CH).astype(F32)
-        branch = dot_nt(act, w_red[...]) + b_red
-        mix = fields[pl.ds(i0, step)].reshape(n, CH).astype(F32) + lscale * branch
-        mix_out[pl.ds(i0, step)] = mix.astype(BF).reshape(step, SIDE, CH)
-        bgrad = (lscale * cot_c).astype(BF)
-        pre_grad = (dot(bgrad, w_red[...]) * slope).astype(BF)
+        pre_grad = (act_grad * (phi + pre * (dens * 0.3989422804014327))).astype(BF)
+        yield
+        ngrad = dot_nt(pre_grad, w_exp[...])
+        branch = dot_nt(act, w_red[...])
         rgrad[...] += dot_tn(bgrad, act)
         egrad[...] += dot_tn(normed, pre_grad)
-        ngrad = dot_nt(pre_grad, w_exp[...]) * gain
+        yield
+        mix = fields[pl.ds(i0, step)].reshape(n, CH).astype(F32) + lscale * (branch + b_red)
+        mix_out[pl.ds(i0, step)] = mix.astype(BF).reshape(step, SIDE, CH)
+        ngrad = ngrad * gain
         m1 = jnp.mean(ngrad, axis=-1, keepdims=True)
         m2 = jnp.mean(ngrad * centred, axis=-1, keepdims=True)
         cgrad = (inv_std * (ngrad - m1 - centred * m2)).astype(BF)
+        yield
         for d in range(step):
             g4[6 + i0 + d] = dot(fwd_g[...], cgrad[d * SIDE : (d + 1) * SIDE])
+        yield
+
+    def chunk(ic, _):
+        gens = [part(pl.multiple_of((ic * parts + k) * step, step)) for k in range(parts)]
+        for tick in range(7 + 1 * (parts - 1)):
+            for k in range(parts):
+                if 0 <= tick - 1 * k < 7:
+                    next(gens[k])
         return 0
 
-    lax.fori_loop(0, SIDE // step, chunk, 0)
+    lax.fori_loop(0, SIDE // (step * parts), chunk, 0)
 
     store_mixed = pltpu.make_async_copy(mix_out, mixed, io_sem.at[1])
     store_mixed.start()
+
+    for g in range(3):
+        lanes = slice(128 * g, 128 * g + 128)
+        wsrc[192 * g : 192 * g + 192] = egrad[:, lanes].astype(BF)
+        wsrc[576 + 192 * g : 768 + 192 * g] = rgrad[:, lanes].astype(BF)
+
+    def dp_block(to):
+        return wsrc.at[pl.ds(pl.multiple_of(to * dp_rows, 16), dp_rows)]
+
+    ca = exchange("dp", ndp, dp_block, lambda m: wa.at[m], sa, ra)
+    wa[md] = wsrc[pl.ds(pl.multiple_of(md * dp_rows, 16), dp_rows)]
+
+    for l0, lw in LANES:
+        for fb in range(5):
+            rows = [slice(40 * t + 8 * fb, 40 * t + 8 * fb + 8) for t in range(3)]
+            lanes = slice(l0, l0 + lw)
+
+            kk = [
+                [kf[u, 120 + 40 * t + 8 * fb : 128 + 40 * t + 8 * fb, lanes] for t in range(3)]
+                for u in range(7)
+            ]
+
+            def pconv(ib, _, fb=fb, rows=rows, lanes=lanes, kk=kk):
+                p0 = ib * 5
+                prods = []
+                for t in range(3):
+                    gs = [g4[p0 + r, rows[t], lanes] for r in range(11)]
+                    back = [k[t] for k in kk][::-1]
+                    prods.append([taps(gs[d : d + 7], back) for d in range(5)])
+                for d in range(5):
+                    y2[p0 + d, 16 * fb : 16 * fb + 16, lanes] = real_imag(*(p[d] for p in prods))
+                return 0
+
+            lax.fori_loop(0, EXT // 5, pconv, 0, unroll=2)
+
+
+    finish(ca)
+    part = wa[0].astype(F32)
+    for j in range(1, ndp):
+        part = part + wa[j].astype(F32)
+    pa[...] = part.reshape(owners, WBLOCK, 128)
+
+    def share(off, src, dst, send, recv):
+        return pltpu.make_async_remote_copy(
+            src_ref=src,
+            dst_ref=dst,
+            send_sem=send.at[off],
+            recv_sem=recv.at[off],
+            device_id={"tile": peer(me, off, TILES)},
+            device_id_type=MESH,
+        )
+
+    def to_owner(off):
+        to = peer(me, off, TILES)
+        return to, share(off, pa.at[lax.rem(to, owners)], wb.at[me], sb, rb)
+
+    for off in range(1, TILES):
+        to, copy = to_owner(off)
+        pl.when(to < owners)(copy.start)
+
+    @pl.when(me < owners)
+    def _():
+        wb[me] = pa[lax.rem(me, owners)]
+
+    for p in range(W):
+        ptop[p] = dot(inv_p[...], y2[p]).astype(BF)
+        pbot[p] = dot(inv_p[...], y2[W + SIDE + p]).astype(BF)
+
+    def from_freq(i, _):
+        back = dot(inv_p[...], y2[i + W])
+        dir_out[i] = (cot[i].astype(F32) + back[0:SIDE]).astype(BF)
+        psides[i] = back[SIDE:].astype(BF)
+        return 0
+
+    lax.fori_loop(0, SIDE, from_freq, 0, unroll=8)
+    store_direct = pltpu.make_async_copy(dir_out, direct, io_sem.at[2])
+    store_direct.start()
+
+    top = ptop[...].reshape(W * KROW, CH)
+    bot = pbot[...].reshape(W * KROW, CH)
+    sides = psides[...].reshape(SIDE * 16, CH)
+
+
+    def take(*parts):
+        total = sum(dot(gather(by_col, name, part.shape[0]), part) for name, part in parts)
+        return total.astype(BF).reshape(1, TILES, CELLS, CH)
+
+    taken = [
+        take(("top0", top)),
+        take(("side1", sides), ("bot1", bot)),
+        take(("bot2", bot)),
+        take(("side3", sides), ("top3", top)),
+    ]
+    pack(own2, jnp.concatenate(taken, axis=0))
+
+
+    c3 = exchange("tile", TILES, lambda to: own2.at[:, to], lambda m: got2.at[:, m], s3, r3)
+    got2[:, me] = own2[:, me]
+    for off in range(1, TILES):
+        to, copy = to_owner(off)
+        pl.when(to < owners)(copy.wait_send)
+        pl.when(me < owners)(copy.wait_recv)
+
+    mine = lax.rem(me, owners)
+
+    @pl.when(me < owners)
+    def _():
+        whole = wb[0]
+        for j in range(1, TILES):
+            whole = whole + wb[j]
+        pc[...] = whole.astype(BF)
+        wc[mine] = whole.astype(BF)
+        for off in range(1, TILES):
+            share(off, pc, wc.at[mine], sc, rc).start()
 
     for l0, lw in LANES:
         for fb in range(5):
@@ -460,124 +625,17 @@
                     m3[u, rows[t], lanes] = accs[7 * t + u]
 
 
-    for g in range(3):
-        lanes = slice(128 * g, 128 * g + 128)
-        wsrc[192 * g : 192 * g + 192] = egrad[:, lanes].astype(BF)
-        wsrc[576 + 192 * g : 768 + 192 * g] = rgrad[:, lanes].astype(BF)
     kg = jnp.concatenate([dot_exact(inv_k[...], m3[u]) for u in range(7)], axis=0)
-    kg = jnp.concatenate([kg, jnp.zeros((8, CH), F32)], axis=0).astype(BF)
-    wsrc[1152:1216] = kg[:, 0:128]
-    wsrc[1216:1280] = jnp.concatenate([kg[:, 128:192], jnp.zeros((64, 64), BF)], axis=1)
-
-    def dp_block(to):
-        return wsrc.at[pl.ds(pl.multiple_of(to * dp_rows, 16), dp_rows)]
-
-    ca = exchange("dp", ndp, dp_block, lambda m: wa.at[m], sa, ra)
-    wa[md] = wsrc[pl.ds(pl.multiple_of(md * dp_rows, 16), dp_rows)]
-
-    for l0, lw in LANES:
-        for fb in range(5):
-            rows = [slice(40 * t + 8 * fb, 40 * t + 8 * fb + 8) for t in range(3)]
-            lanes = slice(l0, l0 + lw)
-
-            kk = [
-                [kf[u, 120 + 40 * t + 8 * fb : 128 + 40 * t + 8 * fb, lanes] for t in range(3)]
-                for u in range(7)
-            ]
-
-            def pconv(ib, _, fb=fb, rows=rows, lanes=lanes, kk=kk):
-                p0 = ib * 5
-                prods = []
-                for t in range(3):
-                    gs = [g4[p0 + r, rows[t], lanes] for r in range(11)]
-                    back = [k[t] for k in kk][::-1]
-                    prods.append([taps(gs[d : d + 7], back) for d in range(5)])
-                for d in range(5):
-                    y2[p0 + d, 16 * fb : 16 * fb + 16, lanes] = real_imag(*(p[d] for p in prods))
-                return 0
-
-            lax.fori_loop(0, EXT // 5, pconv, 0, unroll=2)
-
-
-    finish(ca)
-    part = wa[0].astype(F32)
-    for j in range(1, ndp):
-        part = part + wa[j].astype(F32)
-    pa[...] = part.reshape(owners, WBLOCK, 128)
-
-    def share(off, src, dst, send, recv):
-        return pltpu.make_async_remote_copy(
-            src_ref=src,
-            dst_ref=dst,
-            send_sem=send.at[off],
-            recv_sem=recv.at[off],
-            device_id={"tile": peer(me, off, TILES)},
-            device_id_type=MESH,
-        )
-
-    def to_owner(off):
-        to = peer(me, off, TILES)
-        return to, share(off, pa.at[lax.rem(to, owners)], wb.at[me], sb, rb)
-
-    for off in range(1, TILES):
-        to, copy = to_owner(off)
-        pl.when(to < owners)(copy.start)
-
-    @pl.when(me < owners)
-    def _():
-        wb[me] = pa[lax.rem(me, owners)]
-
-    for p in range(W):
-        ptop[p] = dot(inv_p[...], y2[p]).astype(BF)
-        pbot[p] = dot(inv_p[...], y2[W + SIDE + p]).astype(BF)
-
-    def from_freq(i, _):
-        back = dot(inv_p[...], y2[i + W])
-        direct[i] = (cot[i].astype(F32) + back[0:SIDE]).astype(BF)
-        psides[i] = back[SIDE:].astype(BF)
-        return 0
-
-    lax.fori_loop(0, SIDE, from_freq, 0, unroll=8)
-
-    top = ptop[...].reshape(W * KROW, CH)
-    bot = pbot[...].reshape(W * KROW, CH)
-    sides = psides[...].reshape(SIDE * 16, CH)
-
-
-    def take(*parts):
-        total = sum(dot(gather(by_col, name, part.shape[0]), part) for name, part in parts)
-        return total.astype(BF).reshape(1, TILES, CELLS, CH)
-
-    taken = [
-        take(("top0", top)),
-        take(("side1", sides), ("bot1", bot)),
-        take(("bot2", bot)),
-        take(("side3", sides), ("top3", top)),
-    ]
-    pack(own2, jnp.concatenate(taken, axis=0))
-
-
-    c3 = exchange("tile", TILES, lambda to: own2.at[:, to], lambda m: got2.at[:, m], s3, r3)
-    got2[:, me] = own2[:, me]
-    for off in range(1, TILES):
-        to, copy = to_owner(off)
-        pl.when(to < owners)(copy.wait_send)
-        pl.when(me < owners)(copy.wait_recv)
-
-    mine = lax.rem(me, owners)
-
-    @pl.when(me < owners)
-    def _():
-        whole = wb[0]
-        for j in range(1, TILES):
-            whole = whole + wb[j]
-        pc[...] = whole.astype(BF)
-        wc[mine] = whole.astype(BF)
-        for off in range(1, TILES):
-            share(off, pc, wc.at[mine], sc, rc).start()
-
-    rows = lax.broadcasted_iota(jnp.int32, (1024, 1024), 0)
-    route_back = (rows == target_row[...]).astype(F32).astype(BF)
+    kg = jnp.concatenate([kg, jnp.zeros((8, CH), F32)], axis=0)
+    ksrc[0:64] = kg[:, 0:128]
+    ksrc[64:128] = jnp.concatenate([kg[:, 128:192], jnp.zeros((64, 64), F32)], axis=1)
+
+    def kernel_block(to):
+        return ksrc.at[pl.ds(pl.multiple_of(to * krows, 16), krows)]
+
+    ka = exchange("dp", ndp, kernel_block, lambda m: kwa.at[m], ska, rka)
+    kwa[md] = ksrc[pl.ds(pl.multiple_of(md * krows, 16), krows)]
+
     for off in range(1, TILES):
         copy = share(off, pc, wc.at[mine], sc, rc)
         pl.when(me < owners)(copy.wait_send)
@@ -588,18 +646,37 @@
     pd[...] = block
     cd = exchange("dp", ndp, lambda to: pd, lambda m: wd.at[m], sd, rd)
     wd[md] = block
+    route_back = route_matrix(base, me, 1)
     finish(c3)
     pack(routed2, dot(route_back, unpack(got2)).astype(BF).reshape(4, TILES, CELLS, CH))
     c4 = exchange("tile", TILES, lambda to: routed2.at[:, to], lambda m: back2.at[:, m], s4, r4)
     back2[:, me] = routed2[:, me]
+
+    finish(ka)
+    part = kwa[0]
+    for j in range(1, ndp):
+        part = part + kwa[j]
+    kpart[...] = part.astype(BF)
+    kb = exchange("tile", TILES, lambda to: kpart, lambda m: kwb.at[m], skb, rkb)
+    kwb[me] = kpart[...]
+    finish(kb)
+    part = kwb[0].astype(F32)
+    for j in range(1, TILES):
+        part = part + kwb[j].astype(F32)
+    kwhole[...] = part.astype(BF)
+    kc = exchange("dp", ndp, lambda to: kwhole, lambda m: kwc.at[m], skc, rkc)
+    kwc[md] = kwhole[...]
     finish(cd)
-    wout[...] = wd[...].reshape(WROWS, 128)
+    wout[0:WROWS] = wd[...].reshape(WROWS, 128)
     finish(c4)
     bands[...] = unpack(back2).reshape(4, 256, CH)
+    finish(kc)
+    wout[WROWS:] = kwc[...].reshape(KROWS, 128)
+    store_direct.wait()
     store_mixed.wait()
 
 
-def main(fields, cotangent, target, params, ndp):
+def main(fields, cotangent, neighbors, rotations, params, ndp):
     index = [jnp.asarray(t) for t in static_tables()]
     tables = [jnp.asarray(t) for t in dft_tables()]
     vm = pl.BlockSpec(memory_space=pltpu.VMEM)
@@ -608,9 +685,10 @@
     sem = pltpu.SemaphoreType.DMA((TILES,))
     sem_dp = pltpu.SemaphoreType.DMA((ndp,))
     dp_rows = WROWS // ndp
+    krows = KROWS // ndp
     owners = dp_rows // WBLOCK
-    targets = [target.reshape(1024, 1), target.reshape(1, 1024)]
-    args = [fields, cotangent, *index, *targets, *tables, *params]
+    offsets = jnp.asarray(OFFSETS, jnp.int32).reshape(8, 1)
+    args = [fields, cotangent, *index, neighbors.T, rotations.T, offsets, *tables, *params]
     field = jax.ShapeDtypeStruct((SIDE, SIDE, CH), BF)
     return pl.pallas_call(
         main_kernel,
@@ -618,10 +696,10 @@
             field,
             field,
             jax.ShapeDtypeStruct((4, 256, CH), BF),
-            jax.ShapeDtypeStruct((WROWS, 128), BF),
+            jax.ShapeDtypeStruct((WROWS + KROWS, 128), BF),
         ),
         in_specs=[vm, hbm] + [vm] * (len(args) - 2),
-        out_specs=(hbm, vm, vm, vm),
+        out_specs=(hbm, hbm, vm, vm),
         scratch_shapes=[
             pltpu.VMEM((EXT, KROW, CH), BF),
             pltpu.VMEM((EXT, 3 * NFREQ, CH), F32),
@@ -648,10 +726,17 @@
             pltpu.VMEM((WBLOCK, 128), BF),
             pltpu.VMEM((owners, WBLOCK, 128), BF),
             pltpu.VMEM((ndp, dp_rows, 128), BF),
-            pltpu.SemaphoreType.DMA((2,)),
+            pltpu.VMEM((KROWS, 128), F32),
+            pltpu.VMEM((ndp, krows, 128), F32),
+            pltpu.VMEM((krows, 128), BF),
+            pltpu.VMEM((TILES, krows, 128), BF),
+            pltpu.VMEM((krows, 128), BF),
+            pltpu.VMEM((ndp, krows, 128), BF),
+            pltpu.VMEM((SIDE, SIDE, CH), BF),
+            pltpu.SemaphoreType.DMA((3,)),
         ]
-        + [sem] * 12
-        + [sem_dp] * 4,
+        + [sem] * 14
+        + [sem_dp] * 8,
         compiler_params=pltpu.CompilerParams(
             collective_id=0, has_side_effects=True, vmem_limit_bytes=62 * 2**20
         ),
@@ -659,60 +744,73 @@
     )(*args)
 
 
-def last_kernel(scale, direct, bands, wsum, by_row, out, kgrad, egrad, rgrad):
-    north = dot(spread(by_row, "north", W * SIDE), bands[0]).reshape(W, SIDE, CH)
-    south = dot(spread(by_row, "south", W * SIDE), bands[2]).reshape(W, SIDE, CH)
-    east = dot(spread(by_row, "east", 1024), bands[1]).reshape(SIDE, 16, CH)
-    west = dot(spread(by_row, "west", 1024), bands[3]).reshape(SIDE, 16, CH)
+def last_kernel(
+    scale, mixed, direct, bands, wsum, by_row, mixed_out, out, kgrad, egrad, rgrad, d, b, w, m, sem
+):
+    load_m = pltpu.make_async_copy(mixed, m, sem.at[0])
+    store_m = pltpu.make_async_copy(m, mixed_out, sem.at[5])
+    load_b = pltpu.make_async_copy(bands, b, sem.at[1])
+    load_w = pltpu.make_async_copy(wsum, w, sem.at[2])
+    load_d = pltpu.make_async_copy(direct, d, sem.at[3])
+    store_d = pltpu.make_async_copy(d, out, sem.at[4])
+    for copy in (load_b, load_m, load_d, load_w):
+        copy.start()
+    load_b.wait()
+    north = dot(spread(by_row, "north", W * SIDE), b[0]).reshape(W, SIDE, CH)
+    south = dot(spread(by_row, "south", W * SIDE), b[2]).reshape(W, SIDE, CH)
+    east = dot(spread(by_row, "east", 1024), b[1]).reshape(SIDE, 16, CH)
+    west = dot(spread(by_row, "west", 1024), b[3]).reshape(SIDE, 16, CH)
     mid = slice(W, SIDE - W)
-    out[mid, 16:48] = direct[mid, 16:48]
-    out[mid, 0:16] = (direct[mid, 0:16].astype(F32) + west[mid]).astype(BF)
-    out[mid, 48:64] = (direct[mid, 48:64].astype(F32) + east[mid]).astype(BF)
+    load_m.wait()
+    store_m.start()
+    load_d.wait()
+    d[mid, 0:16] = (d[mid, 0:16].astype(F32) + west[mid]).astype(BF)
+    d[mid, 48:64] = (d[mid, 48:64].astype(F32) + east[mid]).astype(BF)
     zero = jnp.zeros((W, 32, CH), F32)
     for rows, add in ((slice(0, W), north), (slice(SIDE - W, SIDE), south)):
         more = jnp.concatenate([west[rows], zero, east[rows]], axis=1)
-        out[rows] = (direct[rows].astype(F32) + add + more).astype(BF)
+        d[rows] = (d[rows].astype(F32) + add + more).astype(BF)
+    store_d.start()
+    load_w.wait()
     for g in range(3):
         lanes = slice(128 * g, 128 * g + 128)
-        egrad[:, lanes] = wsum[192 * g : 192 * g + 192].astype(F32) * scale
-        rgrad[:, lanes] = wsum[576 + 192 * g : 768 + 192 * g].astype(F32) * scale
-    low = wsum[1152:1216].astype(F32) * scale
-    high = wsum[1216:1280].astype(F32) * scale
+        egrad[:, lanes] = w[192 * g : 192 * g + 192].astype(F32) * scale
+        rgrad[:, lanes] = w[576 + 192 * g : 768 + 192 * g].astype(F32) * scale
+    low = w[WROWS : WROWS + 64].astype(F32) * scale
+    high = w[WROWS + 64 : WROWS + 128].astype(F32) * scale
     for u in range(7):
         kgrad[u, :, 0:128] = low[8 * u : 8 * u + 7]
         kgrad[u, :, 128:192] = high[8 * u : 8 * u + 7, 0:64]
-
-
-def last(direct, bands, wsum, scale):
+    store_d.wait()
+    store_m.wait()
+
+
+def last(mixed, direct, bands, wsum, scale):
     by_row, _ = static_tables()
     vm = pl.BlockSpec(memory_space=pltpu.VMEM)
+    hbm = pl.BlockSpec(memory_space=pl.ANY)
+    field = jax.ShapeDtypeStruct((SIDE, SIDE, CH), BF)
     return pl.pallas_call(
         functools.partial(last_kernel, scale),
         out_shape=(
-            jax.ShapeDtypeStruct((SIDE, SIDE, CH), BF),
+            field,
+            field,
             jax.ShapeDtypeStruct((7, 7, CH), F32),
             jax.ShapeDtypeStruct((CH, HID), F32),
             jax.ShapeDtypeStruct((CH, HID), F32),
         ),
-        in_specs=[vm] * 4,
-        out_specs=(vm,) * 4,
-        compiler_params=pltpu.CompilerParams(vmem_limit_bytes=24 * 2**20),
+        in_specs=[hbm] * 4 + [vm],
+        out_specs=(hbm, hbm, vm, vm, vm),
+        scratch_shapes=[
+            pltpu.VMEM((SIDE, SIDE, CH), BF),
+            pltpu.VMEM((4, 256, CH), BF),
+            pltpu.VMEM((WROWS + KROWS, 128), BF),
+            pltpu.VMEM((SIDE, SIDE, CH), BF),
+            pltpu.SemaphoreType.DMA((6,)),
+        ],
+        compiler_params=pltpu.CompilerParams(vmem_limit_bytes=62 * 2**20),
         name="last",
-    )(direct, bands, wsum, jnp.asarray(by_row))
-
-
-def routing(neighbors, rotations):
-    me = lax.axis_index("tile")
-    offsets = jnp.array(OFFSETS, jnp.int32)[None, :]
-    side = (rotations + offsets) % 4
-    base = jnp.where(neighbors >= 0, side * 256 + neighbors * CELLS, -(1 << 20)).T
-    right = jnp.where(me >= 7, 11, -(1 << 20))
-    left = jnp.where(me <= 8, 0, -(1 << 20))
-    corner_row = jnp.stack([right, left, right, left])[:, None]
-    cell = jnp.arange(CELLS, dtype=jnp.int32)[None, None, :]
-    edge = base[0:4][:, :, None] + cell
-    corner = (base[4:8] + corner_row)[:, :, None]
-    return jnp.where(cell < 12, edge, jnp.where(cell == 12, corner, -1)).astype(jnp.int32)
+    )(mixed, direct, bands, wsum, jnp.asarray(by_row))
 
 
 def on_device(
@@ -733,7 +831,6 @@
     ndp = lax.axis_size("dp")
     field = fields.reshape(SIDE, SIDE, CH)
     cot = cotangent.reshape(SIDE, SIDE, CH)
-    target = routing(neighbors, rotations)
     params = [
         kernel,
         conv_bias,
@@ -745,9 +842,9 @@
         bias_reduce,
         layer_scale,
     ]
-    mixed, direct, bands, wsum = main(field, cot, target, params, ndp)
+    mixed, direct, bands, wsum = main(field, cot, neighbors, rotations, params, ndp)
     scale = 1.0 / math.sqrt(ndp * TILES * SIDE * SIDE)
-    input_grad, kgrad, egrad, rgrad = last(direct, bands, wsum, scale)
+    mixed, input_grad, kgrad, egrad, rgrad = last(mixed, direct, bands, wsum, scale)
     return (
         mixed.reshape(fields.shape),
         input_grad.reshape(fields.shape),

time: 97.5 us -> 88.4 us (0.907)
  local copies, waits for them, and re-layouts: 6.7 us -> 0 us
  Pallas kernels: 88.8 us -> 87.4 us
  other arithmetic: 1.02 us -> 0 us
    unnamed x11 -> x0, local copies, waits for them, and re-layouts: 4.92 us -> none
    pallas_call x1, Pallas kernels: 86.8 us -> 81.9 us  [main(): pl.pallas_call(main_kernel, out_shape=(field, field, jax.ShapeDtypeStruct...]
    pallas_call x1, Pallas kernels: 2.03 us -> 5.53 us  [last(): pl.pallas_call(functools.partial(last_kernel, scale), out_shape=(field, f...]
    select_n x2 -> x0, local copies, waits for them, and re-layouts: 1.77 us -> none  [routing(): jnp.where(cell < 12, edge, jnp.where(cell == 12, corner, -1))]
where the time goes in v4:
time: 88.4 us; the launch traced here: 88.2 us
  Pallas kernels  87.4 us (99%)
    pallas_call x1, Pallas kernels, main(): pl.pallas_call(main_kernel, out_shape=(field, field, jax.ShapeDtypeStruct...  81.9 us
    pallas_call x1, Pallas kernels, last(): pl.pallas_call(functools.partial(last_kernel, scale), out_shape=(field, f...  5.53 us

profile of v4, /device:TPU:1, one launch (start us, length us, event | category | flops | bytes accessed | tf_op | source)
XLA Modules:
  0.0 88.2 jit_solution(15855722956104479171)
XLA Ops:
  0.6 81.9 %main.1 = (bf16[64,64,192]{2,1,0:T(8,128)(2,1)}, bf16[64,64,192]{2,1,0:T(8,128)(2,1)}, bf16[4,256,192]{2,1,0:T(8,128)(2,1)}, bf16[1280,128]{1,0:T(8,128)(2,1)}) custom-call(bf16[64,64,192]{2,1,0:T(8,128)(2,1)} %bitcast.8, bf16[64,64,192]{2,1,0:T(8,128)(2,1)} %bitcast.9, s32[16,256]{1,0:T(8,128)} %constant.18.clone.by_row, s32[256,128]{1,0:T(8,128)} %constant.19.clone.by_col, ...), custom_call_target="tpu_custom_call" | custom-call | tf_op jit(solution)/shard_map/main/pallas_call | solution.py:693
  82.5 5.5 %last.1 = (bf16[64,64,192]{2,1,0:T(8,128)(2,1)}, bf16[64,64,192]{2,1,0:T(8,128)(2,1)}, f32[7,7,192]{2,1,0:T(8,128)}, f32[192,384]{1,0:T(8,128)}, f32[192,384]{1,0:T(8,128)}) custom-call(bf16[64,64,192]{2,1,0:T(8,128)(2,1)} %get-tuple-element.14.mixed, bf16[64,64,192]{2,1,0:T(8,128)(2,1)} %get-tuple-element.15.direct, ...), custom_call_target="tpu_custom_call" | custom-call | tf_op jit(solution)/shard_map/last/pallas_call | solution.py:793

commit v5 on v4

--- a/solution.py
+++ b/solution.py
@@ -500,6 +500,41 @@
 
     for l0, lw in LANES:
         for fb in range(5):
+            rows = [slice(40 * t + 8 * fb, 40 * t + 8 * fb + 8) for t in range(4)]
+            grow = (rows[0], rows[1], rows[3])
+            lanes = slice(l0, l0 + lw)
+
+            def kgrad(ib, accs, rows=rows, lanes=lanes, grow=grow):
+                i0 = ib * 4
+                accs = list(accs)
+                for t in range(3):
+                    xs = [x3[i0 + r, rows[t], lanes] for r in range(10)]
+                    for d in range(4):
+                        g = g4[6 + i0 + d, grow[t], lanes]
+                        for u in range(7):
+                            accs[7 * t + u] = accs[7 * t + u] + xs[d + u] * g
+                return tuple(accs)
+
+            zero = jnp.zeros((8, lw), F32)
+            accs = lax.fori_loop(0, SIDE // 4, kgrad, (zero,) * 21, unroll=2)
+            for t in range(3):
+                for u in range(7):
+                    m3[u, rows[t], lanes] = accs[7 * t + u]
+
+
+    kg = jnp.concatenate([dot_exact(inv_k[...], m3[u]) for u in range(7)], axis=0)
+    kg = jnp.concatenate([kg, jnp.zeros((8, CH), F32)], axis=0)
+    ksrc[0:64] = kg[:, 0:128]
+    ksrc[64:128] = jnp.concatenate([kg[:, 128:192], jnp.zeros((64, 64), F32)], axis=1)
+
+    def kernel_block(to):
+        return ksrc.at[pl.ds(pl.multiple_of(to * krows, 16), krows)]
+
+    ka = exchange("dp", ndp, kernel_block, lambda m: kwa.at[m], ska, rka)
+    kwa[md] = ksrc[pl.ds(pl.multiple_of(md * krows, 16), krows)]
+
+    for l0, lw in LANES:
+        for fb in range(5):
             rows = [slice(40 * t + 8 * fb, 40 * t + 8 * fb + 8) for t in range(3)]
             lanes = slice(l0, l0 + lw)
 
@@ -550,6 +585,13 @@
     def _():
         wb[me] = pa[lax.rem(me, owners)]
 
+    finish(ka)
+    part = kwa[0]
+    for j in range(1, ndp):
+        part = part + kwa[j]
+    kpart[...] = part.astype(BF)
+    kb = exchange("tile", TILES, lambda to: kpart, lambda m: kwb.at[m], skb, rkb)
+    kwb[me] = kpart[...]
     for p in range(W):
         ptop[p] = dot(inv_p[...], y2[p]).astype(BF)
         pbot[p] = dot(inv_p[...], y2[W + SIDE + p]).astype(BF)
@@ -601,64 +643,6 @@
         for off in range(1, TILES):
             share(off, pc, wc.at[mine], sc, rc).start()
 
-    for l0, lw in LANES:
-        for fb in range(5):
-            rows = [slice(40 * t + 8 * fb, 40 * t + 8 * fb + 8) for t in range(4)]
-            grow = (rows[0], rows[1], rows[3])
-            lanes = slice(l0, l0 + lw)
-
-            def kgrad(ib, accs, rows=rows, lanes=lanes, grow=grow):
-                i0 = ib * 4
-                accs = list(accs)
-                for t in range(3):
-                    xs = [x3[i0 + r, rows[t], lanes] for r in range(10)]
-                    for d in range(4):
-                        g = g4[6 + i0 + d, grow[t], lanes]
-                        for u in range(7):
-                            accs[7 * t + u] = accs[7 * t + u] + xs[d + u] * g
-                return tuple(accs)
-
-            zero = jnp.zeros((8, lw), F32)
-            accs = lax.fori_loop(0, SIDE // 4, kgrad, (zero,) * 21, unroll=2)
-            for t in range(3):
-                for u in range(7):
-                    m3[u, rows[t], lanes] = accs[7 * t + u]
-
-
-    kg = jnp.concatenate([dot_exact(inv_k[...], m3[u]) for u in range(7)], axis=0)
-    kg = jnp.concatenate([kg, jnp.zeros((8, CH), F32)], axis=0)
-    ksrc[0:64] = kg[:, 0:128]
-    ksrc[64:128] = jnp.concatenate([kg[:, 128:192], jnp.zeros((64, 64), F32)], axis=1)
-
-    def kernel_block(to):
-        return ksrc.at[pl.ds(pl.multiple_of(to * krows, 16), krows)]
-
-    ka = exchange("dp", ndp, kernel_block, lambda m: kwa.at[m], ska, rka)
-    kwa[md] = ksrc[pl.ds(pl.multiple_of(md * krows, 16), krows)]
-
-    for off in range(1, TILES):
-        copy = share(off, pc, wc.at[mine], sc, rc)
-        pl.when(me < owners)(copy.wait_send)
-        pl.when(peer(me, TILES - off, TILES) < owners)(copy.wait_recv)
-
-    block = wc[...].reshape(owners * WBLOCK, 128)
-    pd = wa.at[0]
-    pd[...] = block
-    cd = exchange("dp", ndp, lambda to: pd, lambda m: wd.at[m], sd, rd)
-    wd[md] = block
-    route_back = route_matrix(base, me, 1)
-    finish(c3)
-    pack(routed2, dot(route_back, unpack(got2)).astype(BF).reshape(4, TILES, CELLS, CH))
-    c4 = exchange("tile", TILES, lambda to: routed2.at[:, to], lambda m: back2.at[:, m], s4, r4)
-    back2[:, me] = routed2[:, me]
-
-    finish(ka)
-    part = kwa[0]
-    for j in range(1, ndp):
-        part = part + kwa[j]
-    kpart[...] = part.astype(BF)
-    kb = exchange("tile", TILES, lambda to: kpart, lambda m: kwb.at[m], skb, rkb)
-    kwb[me] = kpart[...]
     finish(kb)
     part = kwb[0].astype(F32)
     for j in range(1, TILES):
@@ -666,6 +650,22 @@
     kwhole[...] = part.astype(BF)
     kc = exchange("dp", ndp, lambda to: kwhole, lambda m: kwc.at[m], skc, rkc)
     kwc[md] = kwhole[...]
+    route_back = route_matrix(base, me, 1)
+    finish(c3)
+    pack(routed2, dot(route_back, unpack(got2)).astype(BF).reshape(4, TILES, CELLS, CH))
+    c4 = exchange("tile", TILES, lambda to: routed2.at[:, to], lambda m: back2.at[:, m], s4, r4)
+    back2[:, me] = routed2[:, me]
+
+    for off in range(1, TILES):
+        copy = share(off, pc, wc.at[mine], sc, rc)
+        pl.when(me < owners)(copy.wait_send)
+        pl.when(peer(me, TILES - off, TILES) < owners)(copy.wait_recv)
+
+    block = wc[...].reshape(owners * WBLOCK, 128)
+    pd = wa.at[0]
+    pd[...] = block
+    cd = exchange("dp", ndp, lambda to: pd, lambda m: wd.at[m], sd, rd)
+    wd[md] = block
     finish(cd)
     wout[0:WROWS] = wd[...].reshape(WROWS, 128)
     finish(c4)
@@ -753,7 +753,7 @@
     load_w = pltpu.make_async_copy(wsum, w, sem.at[2])
     load_d = pltpu.make_async_copy(direct, d, sem.at[3])
     store_d = pltpu.make_async_copy(d, out, sem.at[4])
-    for copy in (load_b, load_m, load_d, load_w):
+    for copy in (load_b, load_d, load_w, load_m):
         copy.start()
     load_b.wait()
     north = dot(spread(by_row, "north", W * SIDE), b[0]).reshape(W, SIDE, CH)
@@ -761,8 +761,6 @@
     east = dot(spread(by_row, "east", 1024), b[1]).reshape(SIDE, 16, CH)
     west = dot(spread(by_row, "west", 1024), b[3]).reshape(SIDE, 16, CH)
     mid = slice(W, SIDE - W)
-    load_m.wait()
-    store_m.start()
     load_d.wait()
     d[mid, 0:16] = (d[mid, 0:16].astype(F32) + west[mid]).astype(BF)
     d[mid, 48:64] = (d[mid, 48:64].astype(F32) + east[mid]).astype(BF)
@@ -771,6 +769,8 @@
         more = jnp.concatenate([west[rows], zero, east[rows]], axis=1)
         d[rows] = (d[rows].astype(F32) + add + more).astype(BF)
     store_d.start()
+    load_m.wait()
+    store_m.start()
     load_w.wait()
     for g in range(3):
         lanes = slice(128 * g, 128 * g + 128)

time: 88.4 us -> 87 us (0.984)
  Pallas kernels: 87.4 us -> 85.9 us
    pallas_call x1, Pallas kernels: 81.9 us -> 80.4 us  [main(): pl.pallas_call(main_kernel, out_shape=(field, field, jax.ShapeDtypeStruct...]
where the time goes in v5:
time: 87 us; the launch traced here: 86.8 us
  Pallas kernels  85.9 us (99%)
    pallas_call x1, Pallas kernels, main(): pl.pallas_call(main_kernel, out_shape=(field, field, jax.ShapeDtypeStruct...  80.4 us
    pallas_call x1, Pallas kernels, last(): pl.pallas_call(functools.partial(last_kernel, scale), out_shape=(field, f...  5.58 us

profile of v5, /device:TPU:1, one launch (start us, length us, event | category | flops | bytes accessed | tf_op | source)
XLA Modules:
  0.0 86.8 jit_solution(3176824531480237943)
XLA Ops:
  0.6 80.4 %main.1 = (bf16[64,64,192]{2,1,0:T(8,128)(2,1)}, bf16[64,64,192]{2,1,0:T(8,128)(2,1)}, bf16[4,256,192]{2,1,0:T(8,128)(2,1)}, bf16[1280,128]{1,0:T(8,128)(2,1)}) custom-call(bf16[64,64,192]{2,1,0:T(8,128)(2,1)} %bitcast.8, bf16[64,64,192]{2,1,0:T(8,128)(2,1)} %bitcast.9, s32[16,256]{1,0:T(8,128)} %constant.18.clone.by_row, s32[256,128]{1,0:T(8,128)} %constant.19.clone.by_col, ...), custom_call_target="tpu_custom_call" | custom-call | tf_op jit(solution)/shard_map/main/pallas_call | solution.py:693
  81.0 5.6 %last.1 = (bf16[64,64,192]{2,1,0:T(8,128)(2,1)}, bf16[64,64,192]{2,1,0:T(8,128)(2,1)}, f32[7,7,192]{2,1,0:T(8,128)}, f32[192,384]{1,0:T(8,128)}, f32[192,384]{1,0:T(8,128)}) custom-call(bf16[64,64,192]{2,1,0:T(8,128)(2,1)} %get-tuple-element.14.mixed, bf16[64,64,192]{2,1,0:T(8,128)(2,1)} %get-tuple-element.15.direct, ...), custom_call_target="tpu_custom_call" | custom-call | tf_op jit(solution)/shard_map/last/pallas_call | solution.py:793

commit v6 on v5

--- a/solution.py
+++ b/solution.py
@@ -22,6 +22,7 @@
 BF = jnp.bfloat16
 F32 = jnp.float32
 MESH = pl.DeviceIdType.MESH
+FAR_FIRST = (12, 4, 11, 13, 5, 3, 10, 14, 6, 2, 9, 7, 8, 15, 1)
 WROWS = 1152
 KROWS = 128
 WBLOCK = 16
@@ -208,7 +209,7 @@
 def exchange(axis, n, src_of, dst, send, recv):
     me = lax.axis_index(axis)
     copies = []
-    for off in range(1, n):
+    for off in FAR_FIRST if n == TILES else range(1, n):
         to = peer(me, off, n)
         copy = pltpu.make_async_remote_copy(
             src_ref=src_of(to),
@@ -424,7 +425,7 @@
                     y2[i0 + d, 16 * fb : 16 * fb + 16, lanes] = real_imag(*(p[d] for p in prods))
                 return 0
 
-            lax.fori_loop(0, SIDE // 4, conv, 0, unroll=2)
+            lax.fori_loop(0, SIDE // 4, conv, 0, unroll=4)
 
     load_cot.wait()
     egrad[...] = jnp.zeros_like(egrad)

time: 87 us -> 86.5 us (level)
  no operation moved by 1% of the time
where the time goes in v6:
time: 86.5 us; the launch traced here: 86.3 us
  Pallas kernels  85.5 us (99%)
    pallas_call x1, Pallas kernels, main(): pl.pallas_call(main_kernel, out_shape=(field, field, jax.ShapeDtypeStruct...  79.9 us
    pallas_call x1, Pallas kernels, last(): pl.pallas_call(functools.partial(last_kernel, scale), out_shape=(field, f...  5.58 us

profile of v6, /device:TPU:1, one launch (start us, length us, event | category | flops | bytes accessed | tf_op | source)
XLA Modules:
  0.0 86.3 jit_solution(14306662277219201466)
XLA Ops:
  0.6 79.9 %main.1 = (bf16[64,64,192]{2,1,0:T(8,128)(2,1)}, bf16[64,64,192]{2,1,0:T(8,128)(2,1)}, bf16[4,256,192]{2,1,0:T(8,128)(2,1)}, bf16[1280,128]{1,0:T(8,128)(2,1)}) custom-call(bf16[64,64,192]{2,1,0:T(8,128)(2,1)} %bitcast.8, bf16[64,64,192]{2,1,0:T(8,128)(2,1)} %bitcast.9, s32[16,256]{1,0:T(8,128)} %constant.18.clone.by_row, s32[256,128]{1,0:T(8,128)} %constant.19.clone.by_col, ...), custom_call_target="tpu_custom_call" | custom-call | tf_op jit(solution)/shard_map/main/pallas_call | solution.py:694
  80.6 5.6 %last.1 = (bf16[64,64,192]{2,1,0:T(8,128)(2,1)}, bf16[64,64,192]{2,1,0:T(8,128)(2,1)}, f32[7,7,192]{2,1,0:T(8,128)}, f32[192,384]{1,0:T(8,128)}, f32[192,384]{1,0:T(8,128)}) custom-call(bf16[64,64,192]{2,1,0:T(8,128)(2,1)} %get-tuple-element.14.mixed, bf16[64,64,192]{2,1,0:T(8,128)(2,1)} %get-tuple-element.15.direct, ...), custom_call_target="tpu_custom_call" | custom-call | tf_op jit(solution)/shard_map/last/pallas_call | solution.py:794
